TPU v7x, 768 devices: a whole 4x8x12 slice. The times are simulated.
768 devices in a mesh: member: 8 (over y_lo, core), shard: 96 (over z, x, y_hi).
Axes of the slice: x: 4, y: 8 (y_hi: 2, y_lo: 4; y = y_hi * 4 + y_lo), z: 12, core: 2. Of those that a mesh axis runs over, the one named last changes fastest.
Arguments:
- latents: bfloat16 [16, 12288, 1024], P('member', 'shard'), may hold values from -8 to 8
- queries: bfloat16 [16, 12288, 1024], P('member', 'shard'), may hold values from -48 to 48
- neighbours: int32 [12288, 4], P('shard'), may hold values from 0 to 12287, as said below
- truth: float32 [12288, 100], P('shard'), may hold values from -6 to 6
- area_weight: float32 [12288], P('shard'), may hold values from 0.25 to 2.5
- var_weight: float32 [100], replicated, may hold values from 0.25 to 2.5
- proj_weight: bfloat16 [1024, 100], replicated, may hold values from -0.1875 to 0.1875
Outputs:
- latent_grad: bfloat16 [16, 12288, 1024], P('member', 'shard')
- proj_grad: float32 [1024, 100], replicated
Inputs may be any that keep to these rules, and one draw needn't show every extreme that they name: The neighbours of a point of block s (points s * 128 to (s + 1) * 128 - 1) lie among nodes s * 128 - 32 to (s + 1) * 128 + 31, taken modulo 12288; the first point of each block names both ends of that range.
All inputs are finite; a program needn't handle non-finite values.
Results may differ from a plain program's by a relative error of at most 0.0079.
Values may be sent and summed in bfloat16 or wider, within the bound.
No kernel may reach another device: no remote copies, remote signals or barrier semaphores. Data moves between devices by JAX's collectives and lax.ppermute only.
A program may use at most 32 MiB of HBM per device.

v0:
```python
import math

import jax
import jax.numpy as jnp
from jax import lax
from jax.sharding import PartitionSpec as P

smoothing = 0.25
fairness = 0.95


def padded(block, sides, width):
    for axis, dim in sides:
        count = lax.axis_size(axis)
        forward = [(i, i + 1) for i in range(count - 1)]
        forward.append((count - 1, 0))
        backward = [(target, source) for source, target in forward]
        low = lax.ppermute(
            lax.slice_in_dim(block, block.shape[dim] - width, None, axis=dim), axis, forward
        )
        high = lax.ppermute(lax.slice_in_dim(block, 0, width, axis=dim), axis, backward)
        block = jnp.concatenate([low, block, high], axis=dim)
    return block


def slope(diff):
    return diff * lax.rsqrt(diff * diff + smoothing * smoothing)


def crps_grad(ensemble, own_part, target, weighting):
    count = ensemble.shape[0]
    eps_fair = (1.0 - fairness) / count
    spread = jnp.zeros(own_part.shape, jnp.float32)
    for other in range(count):
        spread = spread + slope(own_part - ensemble[other][None])
    skill = slope(own_part - target[None])
    return weighting[None] * (skill / count - (1.0 - eps_fair) / (count * (count - 1)) * spread)


def local(latents, queries, neighbours, truth, area_weight, var_weight, proj_weight):
    members_here, nodes_here, width = latents.shape
    point_count = queries.shape[1]
    degree = neighbours.shape[1]
    variables = proj_weight.shape[1]
    reach = nodes_here // 4
    score_scale = 1.0 / math.sqrt(width)
    shard_index = lax.axis_index("shard")
    total_nodes = nodes_here * lax.axis_size("shard")
    window = padded(latents, (("shard", 1),), reach)
    local_index = (neighbours - shard_index * nodes_here + reach) % total_nodes
    rows = [jnp.take(window, local_index[:, slot], axis=1) for slot in range(degree)]
    scores = (
        jnp.stack(
            [
                jnp.einsum("mpd,mpd->mp", queries, rows_j, preferred_element_type=jnp.float32)
                for rows_j in rows
            ]
        )
        * score_scale
    )
    attn = jax.nn.softmax(scores, axis=0)
    mixed = queries.astype(jnp.float32)
    for slot in range(degree):
        mixed = mixed + attn[slot][..., None] * rows[slot].astype(jnp.float32)
    mixed = mixed.astype(jnp.bfloat16)
    flat_mixed = mixed.reshape(members_here * point_count, width)
    pred = jnp.dot(flat_mixed, proj_weight, preferred_element_type=jnp.float32).reshape(
        members_here, point_count, variables
    )
    weighting = area_weight[:, None] * var_weight[None, :]
    owner_rows = lax.all_to_all(pred, "member", split_axis=1, concat_axis=0, tiled=True)
    share = point_count // lax.axis_size("member")
    start = lax.axis_index("member") * share
    target = lax.dynamic_slice_in_dim(truth, start, share, 0)
    owner_weight = lax.dynamic_slice_in_dim(weighting, start, share, 0)
    owner_grad = crps_grad(owner_rows, owner_rows, target, owner_weight)
    dpred = lax.all_to_all(
        owner_grad.astype(jnp.bfloat16), "member", split_axis=0, concat_axis=1, tiled=True
    ).astype(owner_grad.dtype)
    grad_b = dpred.astype(jnp.bfloat16)
    flat_grad = grad_b.reshape(members_here * point_count, variables)
    weight_term = lax.dot_general(
        flat_mixed, flat_grad, (((0,), (0,)), ((), ())), preferred_element_type=jnp.float32
    )
    proj_grad = lax.psum(weight_term, ("member", "shard"))
    dmixed = lax.dot_general(
        flat_grad, proj_weight, (((1,), (1,)), ((), ())), preferred_element_type=jnp.float32
    )
    dmixed = dmixed.astype(jnp.bfloat16).reshape(members_here, point_count, width)
    dattn = jnp.stack(
        [
            jnp.einsum("mpd,mpd->mp", dmixed, rows_j, preferred_element_type=jnp.float32)
            for rows_j in rows
        ]
    )
    dscores = attn * (dattn - jnp.sum(attn * dattn, axis=0)[None])
    window_grad = jnp.zeros(window.shape, jnp.float32)
    for slot in range(degree):
        contrib = attn[slot][..., None] * dmixed.astype(jnp.float32) + (
            dscores[slot] * score_scale
        )[..., None] * queries.astype(jnp.float32)
        window_grad = window_grad.at[:, local_index[:, slot]].add(contrib)
    own_grad = window_grad[:, reach : reach + nodes_here]
    lower = window_grad[:, :reach]
    upper = window_grad[:, reach + nodes_here :]
    rims = padded(jnp.stack([lower, upper]).astype(jnp.bfloat16), (("shard", 0),), 2).astype(
        jnp.float32
    )
    from_prev = rims[1]
    from_next = rims[4]
    own_grad = own_grad.at[:, :reach].add(from_prev)
    own_grad = own_grad.at[:, nodes_here - reach :].add(from_next)
    return (own_grad.astype(jnp.bfloat16), proj_grad)


def solution(mesh):
    placed = (
        P("member", "shard", None),
        P("member", "shard", None),
        P("shard", None),
        P("shard", None),
        P("shard"),
        P(),
        P(),
    )
    return jax.shard_map(
        local,
        mesh=mesh,
        in_specs=placed,
        out_specs=(P("member", "shard", None), P()),
        check_vma=False,
    )
```

profile of v0, /device:TPU:1, one launch (start us, length us, event | category | flops | bytes accessed | tf_op | source)
XLA Modules:
  0.0 606.6 jit_solution(2496388562053265137)
XLA Ops:
  7.2 1.1 fusion.34
  8.4 8.3 %collective-permute-start = (bf16[2,32,1024]{2,0,1:T(2,128)(2,1)S(1)}, bf16[2,32,1024]{2,0,1:T(2,128)(2,1)S(1)}, u32[]{:S(2)}, u32[]{:S(2)}) collective-permute-start(bf16[2,32,1024]{2,0,1:T(2,128)(2,1)S(1)} %copy.145), channel_id=1, source_target_pairs={{0,1},{1,2},{2,3},{3,4},{4,5},{5,6},{6,7},{7,8},{8,9},{9,10},{10,1... | collective-permute-start | bytes 393224 | tf_op jit(solution)/shard_map/ppermute | solution.py:18
  16.8 16.2 %collective-permute-start.1 = (bf16[2,32,1024]{2,0,1:T(2,128)(2,1)S(1)}, bf16[2,32,1024]{2,0,1:T(2,128)(2,1)S(1)}, u32[]{:S(2)}, u32[]{:S(2)}) collective-permute-start(bf16[2,32,1024]{2,0,1:T(2,128)(2,1)S(1)} %copy.146), channel_id=1, source_target_pairs={{1,0},{2,1},{3,2},{4,3},{5,4},{6,5},{7,6},{8,7},{9,8},{10,9},{11,1... | collective-permute-start | bytes 393224 | tf_op jit(solution)/shard_map/ppermute | solution.py:21
  33.1 0.7 add_select_fusion
  33.8 0.9 constant_dynamic-slice_fusion
  34.7 0.7 dynamic-slice.14
  35.5 0.3 collective-permute-done
  36.0 0.6 constant_dynamic-update-slice_fusion.1
  36.7 1.6 gather_fusion.3
  38.3 1.6 gather_fusion.2
  40.0 1.6 gather_fusion.1
  41.6 1.6 gather_fusion
  43.2 1.9 fusion.19
  45.2 0.6 copy-done.14
  45.9 0.5 copy-done.6
  46.4 0.7 fusion.6
  47.2 0.3 fusion.26
  47.5 0.8 copy.66
  48.2 5.5 all-to-all-start
  53.8 5.8 all-to-all-done
  59.6 1.1 multiply_convert_fusion
  60.7 4.2 all-to-all-start.1
  64.9 5.1 all-to-all-done.1
  70.1 0.3 convolution_convert_fusion
  70.4 1.6 fusion.15
  72.1 0.6 fusion.14
  72.6 0.8 copy.74
  73.5 1.8 copy.71
  75.3 1.8 copy.72
  77.1 1.8 copy.73
  78.9 0.4 broadcast_in_dim.11
  79.3 12.4 %scatter_fusion = f32[2,192,1024]{2,0,1:T(2,128)S(1)} fusion(f32[2,192,1024]{2,0,1:T(2,128)S(1)} %broadcast_in_dim.11, s32[128]{0:T(128)S(1)} %get-tuple-element.86, f32[128,2,1024]{2,1,0:T(2,128)} %copy.71), kind=kCustom, calls=%fused_computation.4 | custom fusion | flops 262144 | bytes 3146240 | tf_op jit(solution)/shard_map/scatter-add | solution.py:102
  91.7 12.4 %scatter_fusion.1 = f32[2,192,1024]{2,0,1:T(2,128)S(1)} fusion(f32[2,192,1024]{2,0,1:T(2,128)S(1)} %scatter_fusion, s32[128]{0:T(128)S(1)} %get-tuple-element.87, f32[128,2,1024]{2,1,0:T(2,128)} %copy.72), kind=kCustom, calls=%fused_computation.5 | custom fusion | flops 262144 | bytes 3146240 | tf_op jit(solution)/shard_map/scatter-add | solution.py:102
  104.2 12.4 %scatter_fusion.2 = f32[2,192,1024]{2,0,1:T(2,128)S(1)} fusion(f32[2,192,1024]{2,0,1:T(2,128)S(1)} %scatter_fusion.1, s32[128]{0:T(128)S(1)} %get-tuple-element.88, f32[128,2,1024]{2,1,0:T(2,128)} %copy.73), kind=kCustom, calls=%fused_computation.6 | custom fusion | flops 262144 | bytes 3146240 | tf_op jit(solution)/shard_map/scatter-add | solution.py:102
  116.6 6.5 %scatter_fusion.3 = f32[2,192,1024]{2,0,1:T(2,128)S(1)} fusion(f32[2,192,1024]{2,0,1:T(2,128)S(1)} %scatter_fusion.2, s32[128]{0:T(128)S(1)} %get-tuple-element.85, f32[128,2,1024]{2,1,0:T(2,128)S(1)} %copy.74), kind=kCustom, calls=%fused_computation.7 | custom fusion | flops 262144 | bytes 3146240 | tf_op jit(solution)/shard_map/scatter-add | solution.py:102
  123.1 0.5 convert.8
  123.8 1.1 pad_maximum_fusion
  124.9 12.3 %collective-permute-start.3 = (bf16[2,2,32,1024]{3,1,2,0:T(2,128)(2,1)}, bf16[2,2,32,1024]{3,1,2,0:T(2,128)(2,1)}, u32[]{:S(2)}, u32[]{:S(2)}) collective-permute-start(bf16[2,2,32,1024]{3,1,2,0:T(2,128)(2,1)} %pad_maximum_fusion), channel_id=1, source_target_pairs={{1,0},{2,1},{3,2},{4,3},{5,4},{6,5},{7,6},{8,7},{9,8},{10,9},{11,1... | collective-permute-start | bytes 786440 | tf_op jit(solution)/shard_map/ppermute | solution.py:21
  137.2 1.9 collective-permute-start.2
  139.2 1.0 fusion.37
  140.3 2.8 collective-permute-done.3
  143.1 14.6 %collective-permute-done.2 = bf16[2,2,32,1024]{3,1,2,0:T(2,128)(2,1)} collective-permute-done((bf16[2,2,32,1024]{3,1,2,0:T(2,128)(2,1)}, bf16[2,2,32,1024]{3,1,2,0:T(2,128)(2,1)}, u32[]{:S(2)}, u32[]{:S(2)}) %collective-permute-start.2) | collective-permute-done | bytes 262176 | tf_op jit(solution)/shard_map/ppermute | solution.py:18
  157.7 1.1 fusion.25
  158.8 1.2 fusion.23
  160.0 0.4 convert_element_type.53
  160.4 0.9 copy.75
  161.3 436.7 %all-reduce.2.cloned.1.call-done = f32[1024,100]{0,1:T(8,128)} async-done(((f32[1024,100]{0,1:T(8,128)}), f32[1024,100]{0,1:T(8,128)}) %all-reduce.2.cloned.1.call-update) | async-done | bytes 409616 | tf_op jit(solution)/shard_map/psum | solution.py:85
  598.0 1.8 copy.156
  (65 shorter events, 1.2 us)
Async XLA Ops:
  7.2 40.0 %copy-start = (bf16[1024,100]{0,1:T(8,128)(2,1)S(1)}, bf16[1024,100]{0,1:T(8,128)(2,1)}, u32[]{:S(2)}) copy-start(bf16[1024,100]{0,1:T(8,128)(2,1)} %param.19) | copy-start | bytes 614404
  7.2 28.8 %copy-start.3 = (bf16[2,128,1024]{2,1,0:T(8,128)(2,1)S(1)}, bf16[2,128,1024]{2,1,0:T(8,128)(2,1)}, u32[]{:S(2)}) copy-start(bf16[2,128,1024]{2,1,0:T(8,128)(2,1)} %param.13) | copy-start | bytes 1572868
  8.4 27.5 %collective-permute-start = (bf16[2,32,1024]{2,0,1:T(2,128)(2,1)S(1)}, bf16[2,32,1024]{2,0,1:T(2,128)(2,1)S(1)}, u32[]{:S(2)}, u32[]{:S(2)}) collective-permute-start(bf16[2,32,1024]{2,0,1:T(2,128)(2,1)S(1)} %copy.145), channel_id=1, source_target_pairs={{0,1},{1,2},{2,3},{3,4},{4,5},{5,6},{6,7},{7,8},{8,9},{9,10},{10,1... | collective-permute-start | bytes 393224 | tf_op jit(solution)/shard_map/ppermute | solution.py:18
  16.8 19.7 %collective-permute-start.1 = (bf16[2,32,1024]{2,0,1:T(2,128)(2,1)S(1)}, bf16[2,32,1024]{2,0,1:T(2,128)(2,1)S(1)}, u32[]{:S(2)}, u32[]{:S(2)}) collective-permute-start(bf16[2,32,1024]{2,0,1:T(2,128)(2,1)S(1)} %copy.146), channel_id=1, source_target_pairs={{1,0},{2,1},{3,2},{4,3},{5,4},{6,5},{7,6},{8,7},{9,8},{10,9},{11,1... | collective-permute-start | bytes 393224 | tf_op jit(solution)/shard_map/ppermute | solution.py:21
  33.8 12.1 %copy-start.16 = (pred[128]{0:T(512)(128)(4,1)}, pred[128]{0:T(512)(128)(4,1)S(1)}, u32[]{:S(2)}) copy-start(pred[128]{0:T(512)(128)(4,1)S(1)} %get-tuple-element.45) | copy-start | bytes 388
  33.8 12.1 %copy-start.17 = (pred[128]{0:T(512)(128)(4,1)}, pred[128]{0:T(512)(128)(4,1)S(1)}, u32[]{:S(2)}) copy-start(pred[128]{0:T(512)(128)(4,1)S(1)} %get-tuple-element.89) | copy-start | bytes 388
  33.8 12.1 %copy-start.18 = (pred[128]{0:T(512)(128)(4,1)}, pred[128]{0:T(512)(128)(4,1)S(1)}, u32[]{:S(2)}) copy-start(pred[128]{0:T(512)(128)(4,1)S(1)} %get-tuple-element.91) | copy-start | bytes 388
  33.8 12.1 %copy-start.19 = (pred[128]{0:T(512)(128)(4,1)}, pred[128]{0:T(512)(128)(4,1)S(1)}, u32[]{:S(2)}) copy-start(pred[128]{0:T(512)(128)(4,1)S(1)} %get-tuple-element.93) | copy-start | bytes 388
  43.2 3.2 copy-start.1
  45.2 0.6 copy-start.14
  45.2 0.6 copy-start.4
  45.8 0.6 copy-start.6
  45.8 0.6 copy-start.8
  45.8 0.6 copy-start.10
  45.9 0.6 copy-start.12
  46.4 7.3 %copy-start.20 = (f32[100]{0:T(128)S(1)}, f32[100]{0:T(128)}, u32[]{:S(2)}) copy-start(f32[100]{0:T(128)} %param.18) | copy-start | bytes 1204
  48.2 11.3 %all-to-all-start = ((f32[2,128,100]{2,0,1:T(2,128)}), f32[2,128,100]{2,0,1:T(2,128)S(1)}, u32[]{:S(2)}, u32[]{:S(2)}) async-start(f32[2,128,100]{2,0,1:T(2,128)} %copy.66), calls=%async_computation | async-start | bytes 262144 | tf_op jit(solution)/shard_map/all_to_all | solution.py:71
  60.7 9.3 %all-to-all-start.1 = ((bf16[16,16,100]{2,1,0:T(8,128)(2,1)}), bf16[16,16,100]{2,1,0:T(8,128)(2,1)S(1)}, u32[]{:S(2)}, u32[]{:S(2)}) async-start(bf16[16,16,100]{2,1,0:T(8,128)(2,1)} %multiply_convert_fusion), calls=%async_computation.1 | async-start | bytes 131072 | tf_op jit(solution)/shard_map/all_to_all | solution.py:77
  64.9 533.1 %all-reduce.2.cloned.1.call-start = ((), (), s32[]{:S(2)}) async-start(), calls=%async_computation.2 | async-start | bytes 851968 | tf_op jit(solution)/shard_map/psum | solution.py:85
  70.0 1.9 copy-start.5
  70.0 1.9 copy-start.15
  70.0 2.0 copy-start.7
  70.1 2.0 copy-start.9
  70.1 2.0 copy-start.11
  70.1 2.0 copy-start.13
  123.8 13.4 %copy-start.2 = (bf16[1,2,32,1024]{3,1,2,0:T(2,128)(2,1)}, bf16[1,2,32,1024]{3,1,2,0:T(2,128)(2,1)S(1)}, u32[]{:S(2)}) copy-start(bf16[1,2,32,1024]{3,1,2,0:T(2,128)(2,1)S(1)} %get-tuple-element.58) | copy-start | bytes 393220
  124.9 18.2 %collective-permute-start.3 = (bf16[2,2,32,1024]{3,1,2,0:T(2,128)(2,1)}, bf16[2,2,32,1024]{3,1,2,0:T(2,128)(2,1)}, u32[]{:S(2)}, u32[]{:S(2)}) collective-permute-start(bf16[2,2,32,1024]{3,1,2,0:T(2,128)(2,1)} %pad_maximum_fusion), channel_id=1, source_target_pairs={{1,0},{2,1},{3,2},{4,3},{5,4},{6,5},{7,6},{8,7},{9,8},{10,9},{11,1... | collective-permute-start | bytes 786440 | tf_op jit(solution)/shard_map/ppermute | solution.py:21
  137.2 20.4 %collective-permute-start.2 = (bf16[2,2,32,1024]{3,1,2,0:T(2,128)(2,1)}, bf16[2,2,32,1024]{3,1,2,0:T(2,128)(2,1)}, u32[]{:S(2)}, u32[]{:S(2)}) collective-permute-start(bf16[2,2,32,1024]{3,1,2,0:T(2,128)(2,1)} %pad_maximum_fusion), channel_id=1, source_target_pairs={{0,1},{1,2},{2,3},{3,4},{4,5},{5,6},{6,7},{7,8},{8,9},{9,10},{10,1... | collective-permute-start | bytes 786440 | tf_op jit(solution)/shard_map/ppermute | solution.py:18
Sparse Core Ops, SparseCore 0:
  140.4 457.5 all-reduce.1
where the time goes:
time: 608 us; the launch traced here: 607 us
  waiting for transfers between devices  465 us (76%)
  other arithmetic  54.9 us (9%)
  starting transfers between devices  48.4 us (8%)
  local copies, waits for them, and re-layouts  21.9 us (4%)
  between operations  14.6 us (2%)
    psum x1, waiting for transfers between devices, local(): proj_grad = lax.psum(weight_term, ('member', 'shard'))  437 us
    scatter-add x4, other arithmetic, local(): window_grad = window_grad.at[:, local_index[:, slot]].add(contrib)  43.7 us
    ppermute x2, starting transfers between devices, padded(): lax.ppermute(lax.slice_in_dim(block, 0, width, axis=dim), axis, backward)  28.5 us
    ppermute x2, waiting for transfers between devices, padded(): lax.ppermute(lax.slice_in_dim(block, block.shape[dim] - width, None, axis...  14.9 us
  transfers between devices with their start and end apart: 7, of which 6 were waited for; matrix products, arithmetic and copies ran while one was open for 1% of the time, Pallas kernels for 0%

commit v1 on v0

v1 whole, which is shorter than its diff:
```python
import functools
import math

import jax
import jax.numpy as jnp
from jax import lax
from jax.experimental import pallas as pl
from jax.experimental.pallas import tpu as pltpu
from jax.sharding import Mesh, PartitionSpec as P

smoothing = 0.25
fairness = 0.95
LANES = 128
f32, bf16 = jnp.float32, jnp.bfloat16

MEMBER = ("ylo", "core")
SHARD = ("z", "x", "yhi")
SPREAD = ("x", "ylo", "core")
VMEM_LIMIT = 48 * 1024 * 1024


def slope(diff):
    return diff * lax.rsqrt(diff * diff + smoothing * smoothing)


def dot(a, b, ca, cb):
    return lax.dot_general(a, b, (((ca,), (cb,)), ((), ())), preferred_element_type=f32)


def halves(x):
    high = x.astype(bf16)
    return high, (x - high.astype(f32)).astype(bf16)


def fill_window(window, m, own, low, high):
    nodes, reach = own.shape[1], low.shape[1]
    window[0:nodes] = own[m]
    window[nodes : nodes + reach] = low[m]
    window[nodes + reach : nodes + 2 * reach] = high[m]


def forward_kernel(
    scale, slots, own, low, high, queries, weight, attn_out, mixed_out, pred_out, window
):
    members, points, _ = queries.shape
    rows = window.shape[0]
    nodes, reach = own.shape[1], low.shape[1]
    share = pred_out.shape[2]
    window[nodes + 2 * reach :] = jnp.zeros((rows - nodes - 2 * reach, window.shape[1]), bf16)
    place = lax.broadcasted_iota(jnp.int32, (rows, points), 0)
    count = jnp.zeros((rows, points), f32)
    for slot in range(slots.shape[0]):
        count = count + (place == slots[slot : slot + 1]).astype(f32)
    used = count > 0.0
    for m in range(members):
        fill_window(window, m, own, low, high)
        scores = dot(window[...], queries[m], 1, 1) * scale
        scores = jnp.where(used, scores, -1e30)
        top = jnp.max(scores, axis=0, keepdims=True)
        raised = count * jnp.exp(scores - top)
        attn = raised / jnp.sum(raised, axis=0, keepdims=True)
        attn_out[m] = attn
        attn_high, attn_low = halves(attn)
        mixed = queries[m].astype(f32) + (
            dot(attn_high, window[...], 0, 0) + dot(attn_low, window[...], 0, 0)
        )
        mixed = mixed.astype(bf16)
        mixed_out[m] = mixed
        pred = dot(mixed, weight[...], 1, 1)
        for k in range(points // share):
            pred_out[k, m] = pred[k * share : (k + 1) * share]


def crps_kernel(rows, target, weighting, out):
    groups, each, share, lanes = rows.shape
    count = groups * each
    eps_fair = (1.0 - fairness) / count
    values = [rows[k // each, k % each] for k in range(count)]
    spread = [jnp.zeros((share, lanes), f32) for _ in range(count)]
    for a in range(count):
        for b in range(a + 1, count):
            s = slope(values[a] - values[b])
            spread[a] = spread[a] + s
            spread[b] = spread[b] - s
    for k in range(count):
        skill = slope(values[k] - target[...])
        grad = weighting[...] * (
            skill / count - (1.0 - eps_fair) / (count * (count - 1)) * spread[k]
        )
        out[k // each, k % each] = grad.astype(bf16)


def weight_kernel(grads, mixed, out):
    owners, members, share, lanes = grads.shape
    points = owners * share
    total = None
    for m in range(members):
        g = grads[:, m].reshape(points, lanes)
        term = dot(g, mixed[m], 0, 0)
        total = term if total is None else total + term
    pieces, high, wide = out.shape
    across = total.shape[1] // wide
    for k in range(pieces):
        r, c = k // across * high, k % across * wide
        out[k] = total[r : r + high, c : c + wide].astype(bf16)


def backward_kernel(
    scale, grads, attn, own, low, high, queries, weight, own_out, low_out, high_out, window
):
    owners, members, share, lanes = grads.shape
    points = owners * share
    rows = window.shape[0]
    nodes, reach = own.shape[1], low.shape[1]
    window[nodes + 2 * reach :] = jnp.zeros((rows - nodes - 2 * reach, window.shape[1]), bf16)
    for m in range(members):
        fill_window(window, m, own, low, high)
        g = grads[:, m].reshape(points, lanes)
        dmixed = dot(g, weight[...], 1, 0).astype(bf16)
        dattn = dot(window[...], dmixed, 1, 1)
        a = attn[m]
        dscores = a * (dattn - jnp.sum(a * dattn, axis=0, keepdims=True)) * scale
        a_high, a_low = halves(a)
        s_high, s_low = halves(dscores)
        total = (
            dot(a_high, dmixed, 1, 0)
            + dot(s_high, queries[m], 1, 0)
            + dot(a_low, dmixed, 1, 0)
            + dot(s_low, queries[m], 1, 0)
        )
        own_out[m] = total[:nodes]
        low_out[m] = total[nodes : nodes + reach].astype(bf16)
        high_out[m] = total[nodes + reach : nodes + 2 * reach].astype(bf16)


def finish_kernel(own, from_prev, from_next, out):
    nodes, reach = own.shape[1], from_prev.shape[1]
    for m in range(own.shape[0]):
        out[m, :reach] = (own[m, :reach] + from_prev[m].astype(f32)).astype(bf16)
        out[m, reach : nodes - reach] = own[m, reach : nodes - reach].astype(bf16)
        out[m, nodes - reach :] = (own[m, nodes - reach :] + from_next[m].astype(f32)).astype(bf16)


def call(kernel, out_shape, args, scratch=(), name=None):
    vmem = pl.BlockSpec(memory_space=pltpu.VMEM)
    single = not isinstance(out_shape, (list, tuple))
    return pl.pallas_call(
        kernel,
        out_shape=out_shape,
        in_specs=[vmem] * len(args),
        out_specs=vmem if single else [vmem] * len(out_shape),
        scratch_shapes=list(scratch),
        compiler_params=pltpu.CompilerParams(vmem_limit_bytes=VMEM_LIMIT),
        name=name,
    )(*args)


def spread_out(x, axes):
    count = lax.axis_size(axes)
    return lax.all_to_all(jnp.broadcast_to(x[None], (count,) + x.shape), axes, 0, 0, tiled=True)


def local(latents, queries, neighbours, truth, area_weight, var_weight, proj_weight):
    members, nodes, width = latents.shape
    points = queries.shape[1]
    variables = proj_weight.shape[1]
    reach = nodes // 4
    scale = 1.0 / math.sqrt(width)
    shards = lax.axis_size(SHARD)
    owners = lax.axis_size(MEMBER)
    share = points // owners
    forward = [(i, (i + 1) % shards) for i in range(shards)]
    backward = [(i, (i - 1) % shards) for i in range(shards)]

    low = lax.ppermute(latents[:, nodes - reach :], SHARD, forward)
    high = lax.ppermute(latents[:, :reach], SHARD, backward)

    first = lax.axis_index(SHARD) * nodes
    index = (neighbours.T - first + reach) % (nodes * shards)
    slots = jnp.where(
        index < reach, index + nodes, jnp.where(index < nodes + reach, index - reach, index)
    )
    weight = jnp.pad(proj_weight.T, ((0, LANES - variables), (0, 0)))
    start = lax.axis_index(MEMBER) * share
    pad_lanes = ((0, 0), (0, LANES - variables))
    target = jnp.pad(lax.dynamic_slice_in_dim(truth, start, share, 0), pad_lanes)
    area = lax.dynamic_slice_in_dim(area_weight, start, share, 0)
    weighting = jnp.pad(area[:, None] * var_weight[None, :], pad_lanes)

    window_rows = 2 * LANES
    window = pltpu.VMEM((window_rows, width), bf16)
    attn, mixed, pred = call(
        functools.partial(forward_kernel, scale),
        [
            jax.ShapeDtypeStruct((members, window_rows, points), f32),
            jax.ShapeDtypeStruct((members, points, width), bf16),
            jax.ShapeDtypeStruct((owners, members, share, LANES), f32),
        ],
        (slots, latents, low, high, queries, weight),
        [window],
        name="forward",
    )
    rows = lax.all_to_all(pred, MEMBER, 0, 0, tiled=True)
    owner_grad = call(
        crps_kernel,
        jax.ShapeDtypeStruct(rows.shape, bf16),
        (rows, target, weighting),
        name="crps",
    )
    grads = lax.all_to_all(owner_grad, MEMBER, 0, 0, tiled=True)

    across = width // LANES
    pieces = lax.axis_size(SPREAD)
    tall = LANES // (pieces // across)
    term = call(
        weight_kernel,
        jax.ShapeDtypeStruct((pieces, tall, LANES), bf16),
        (grads, mixed),
        name="weight_term",
    )
    term = lax.all_to_all(term, SPREAD, 0, 0, tiled=True)

    own_part, low_part, high_part = call(
        functools.partial(backward_kernel, scale),
        [
            jax.ShapeDtypeStruct((members, nodes, width), f32),
            jax.ShapeDtypeStruct((members, reach, width), bf16),
            jax.ShapeDtypeStruct((members, reach, width), bf16),
        ],
        (grads, attn, latents, low, high, queries, weight),
        [window],
        name="backward",
    )
    term, low_part, high_part = lax.optimization_barrier((term, low_part, high_part))
    from_next = lax.ppermute(low_part, SHARD, backward)
    from_prev = lax.ppermute(high_part, SHARD, forward)

    piece = jnp.sum(term.astype(f32), axis=0).astype(bf16)
    piece = jnp.sum(spread_out(piece, "z").astype(f32), axis=0)
    piece = piece + lax.ppermute(piece, "yhi", [(0, 1), (1, 0)])
    piece, from_next, from_prev = lax.optimization_barrier((piece, from_next, from_prev))
    full = spread_out(piece.astype(bf16), SPREAD).astype(f32)
    full = full.reshape(pieces // across, across, tall, LANES).transpose(0, 2, 1, 3)
    proj_grad = full.reshape(LANES, width)[:variables].T

    latent_grad = call(
        finish_kernel,
        jax.ShapeDtypeStruct(latents.shape, bf16),
        (own_part, from_prev, from_next),
        name="finish",
    )
    return latent_grad, proj_grad


def solution(mesh):
    fine = Mesh(mesh.devices.reshape(4, 2, 12, 4, 2), MEMBER + SHARD)
    placed = (
        P(MEMBER, SHARD, None),
        P(MEMBER, SHARD, None),
        P(SHARD, None),
        P(SHARD, None),
        P(SHARD),
        P(),
        P(),
    )
    return jax.shard_map(
        local,
        mesh=fine,
        in_specs=placed,
        out_specs=(P(MEMBER, SHARD, None), P()),
        check_vma=False,
    )
```

time: 608 us -> 123 us (0.20)
  waiting for transfers between devices: 465 us -> 44.8 us
  other arithmetic: 54.9 us -> 0.97 us
  local copies, waits for them, and re-layouts: 21.9 us -> 5 us
  between operations: 14.6 us -> 0.81 us
  blocking collectives: 0 us -> 8.5 us
  Pallas kernels: 0 us -> 7.76 us
  starting transfers between devices: 48.4 us -> 54.9 us
    psum x1 -> x0, waiting for transfers between devices: 437 us -> none  [local(): proj_grad = lax.psum(weight_term, ('member', 'shard'))]
    scatter-add x6 -> x0, other arithmetic: 46.1 us -> none  [the longest x4 43.7 us: local(): window_grad = window_grad.at[:, local_index[:, slot]].add(contrib)]
    all_to_all x2 -> x4, waiting for transfers between devices: 10.9 us -> 24.4 us  [the longest x2 11.8 us: spread_out(): lax.all_to_all(jnp.broadcast_to(x[None], (count,) + x.shape), axes, 0, 0,...]
    all_to_all x2 -> x4, starting transfers between devices: 9.68 us -> 18.9 us  [the longest x2 9.2 us: spread_out(): lax.all_to_all(jnp.broadcast_to(x[None], (count,) + x.shape), axes, 0, 0,...]
    all_to_all x0 -> x1, blocking collectives: none -> 8.5 us  [local(): grads = lax.all_to_all(owner_grad, MEMBER, 0, 0, tiled=True)]
    pallas_call x0 -> x5, Pallas kernels: none -> 7.76 us  [call(): pl.pallas_call(kernel, out_shape=out_shape, in_specs=[vmem] * len(args),...]
    gather x4 -> x0, local copies, waits for them, and re-layouts: 6.51 us -> none  [local(): jnp.take(window, local_index[:, slot], axis=1)]
    add x4 -> x0, local copies, waits for them, and re-layouts: 6.25 us -> none  [local(): attn[slot][..., None] * dmixed.astype(jnp.float32)]
  transfers between devices with their start and end apart: 7 -> 9, of which waited for: 6 -> 7; matrix products, arithmetic and copies ran while one was open for 1% -> 1% of each run, Pallas kernels for 0% -> 3%
where the time goes in v1:
time: 123 us
  starting transfers between devices  54.9 us (45%)
  waiting for transfers between devices  44.8 us (36%)
  blocking collectives  8.5 us (7%)
  Pallas kernels  7.76 us (6%)
  local copies, waits for them, and re-layouts  5 us (4%)
    ppermute x1, starting transfers between devices, local(): high = lax.ppermute(latents[:, :reach], SHARD, backward)  22.6 us
    ppermute x1, waiting for transfers between devices, local(): low = lax.ppermute(latents[:, nodes - reach:], SHARD, forward)  12.5 us
    all_to_all x2, waiting for transfers between devices, spread_out(): lax.all_to_all(jnp.broadcast_to(x[None], (count,) + x.shape), axes, 0, 0,...  11.8 us
    all_to_all x2, starting transfers between devices, spread_out(): lax.all_to_all(jnp.broadcast_to(x[None], (count,) + x.shape), axes, 0, 0,...  9.2 us
    all_to_all x1, blocking collectives, local(): grads = lax.all_to_all(owner_grad, MEMBER, 0, 0, tiled=True)  8.5 us
    all_to_all x1, waiting for transfers between devices, local(): term = lax.all_to_all(term, SPREAD, 0, 0, tiled=True)  8.28 us
    pallas_call x5, Pallas kernels, call(): pl.pallas_call(kernel, out_shape=out_shape, in_specs=[vmem] * len(args),...  7.76 us
    ppermute x1, waiting for transfers between devices, local(): piece = piece + lax.ppermute(piece, 'yhi', [(0, 1), (1, 0)])  7.29 us
  transfers between devices with their start and end apart: 9, of which 7 were waited for; matrix products, arithmetic and copies ran while one was open for 1% of the time, Pallas kernels for 3%

profile of v1, /device:TPU:1, one launch (start us, length us, event | category | flops | bytes accessed | tf_op | source)
XLA Modules:
  0.0 122.7 jit_solution(12663710696686354443)
XLA Ops:
  0.6 0.0 copy-start
  0.6 0.0 copy-start.1
  0.7 0.0 copy-start.2
  0.7 1.1 fusion.2
  1.7 22.6 %collective-permute-start.1 = (bf16[2,32,1024]{2,1,0:T(8,128)(2,1)S(1)}, bf16[2,32,1024]{2,1,0:T(8,128)(2,1)S(1)}, u32[]{:S(2)}, u32[]{:S(2)}) collective-permute-start(bf16[2,32,1024]{2,1,0:T(8,128)(2,1)S(1)} %get-tuple-element.26), channel_id=1, source_target_pairs={{0,95},{1,0},{2,1},{3,2},{4,3},{5,4},{6,5},{7,6},{8,7},{9,8},{10,9... | collective-permute-start | bytes 393224 | tf_op jit(solution)/shard_map/ppermute | solution.py:176
  24.3 1.9 %collective-permute-start = (bf16[2,32,1024]{2,1,0:T(8,128)(2,1)S(1)}, bf16[2,32,1024]{2,1,0:T(8,128)(2,1)S(1)}, u32[]{:S(2)}, u32[]{:S(2)}) collective-permute-start(bf16[2,32,1024]{2,1,0:T(8,128)(2,1)S(1)} %get-tuple-element.27), channel_id=1, source_target_pairs={{0,1},{1,2},{2,3},{3,4},{4,5},{5,6},{6,7},{7,8},{8,9},{9,10},{10,1... | collective-permute-start | bytes 393224 | tf_op jit(solution)/shard_map/ppermute | solution.py:175
  26.3 0.0 copy-start.3
  26.3 1.0 pad.11.weight
  27.3 0.0 copy-done.3
  27.3 0.0 collective-permute-done.1.high
  27.3 12.5 %collective-permute-done.low = bf16[2,32,1024]{2,1,0:T(8,128)(2,1)S(1)} collective-permute-done((bf16[2,32,1024]{2,1,0:T(8,128)(2,1)S(1)}, bf16[2,32,1024]{2,1,0:T(8,128)(2,1)S(1)}, u32[]{:S(2)}, u32[]{:S(2)}) %collective-permute-start) | collective-permute-done | bytes 131104 | tf_op jit(solution)/shard_map/ppermute | solution.py:175
  39.9 0.0 copy-done.1
  39.9 0.0 copy-done.2
  39.9 2.5 %forward.1 = (f32[2,256,128]{2,1,0:T(8,128)S(1)}, bf16[2,128,1024]{2,1,0:T(8,128)(2,1)S(1)}, f32[8,2,16,128]{3,2,1,0:T(8,128)}) custom-call(s32[4,128]{1,0:T(4,128)S(1)} %fusion.slots, bf16[2,128,1024]{2,1,0:T(8,128)(2,1)S(1)} %copy-done.1, bf16[2,32,1024]{2,1,0:T(8,128)(2,1)S(1)} %collective-permute-done.low, ...), custom_call_target="tpu_custom_call" | custom-call | tf_op jit(solution)/shard_map/forward/pallas_call | solution.py:147
  42.4 5.4 %all-to-all-start = ((f32[8,2,16,128]{3,2,1,0:T(8,128)}), f32[8,2,16,128]{3,2,1,0:T(8,128)S(1)}, u32[]{:S(2)}, u32[]{:S(2)}) async-start(f32[8,2,16,128]{3,2,1,0:T(8,128)} %get-tuple-element.14), calls=%async_computation | async-start | bytes 262144 | tf_op jit(solution)/shard_map/all_to_all | solution.py:203
  47.7 0.0 copy-done
  47.7 0.0 copy-start.5
  47.7 0.1 constant_dynamic-slice_fusion
  47.8 0.6 copy-done.5
  48.4 0.1 dynamic_slice.7
  48.5 0.0 copy-start.4
  48.5 0.1 copy.15
  48.5 0.6 copy-done.4
  49.1 0.1 broadcast_multiply_fusion
  49.2 4.4 %all-to-all-done.rows = f32[8,2,16,128]{3,2,1,0:T(8,128)S(1)} async-done(((f32[8,2,16,128]{3,2,1,0:T(8,128)}), f32[8,2,16,128]{3,2,1,0:T(8,128)S(1)}, u32[]{:S(2)}, u32[]{:S(2)}) %all-to-all-start) | async-done | bytes 131104 | tf_op jit(solution)/shard_map/all_to_all | solution.py:203
  53.6 0.3 crps.1
  53.9 8.5 %all_to_all.25.grads = bf16[8,2,16,128]{3,2,1,0:T(8,128)(2,1)S(1)} all-to-all(bf16[8,2,16,128]{3,2,1,0:T(8,128)(2,1)S(1)} %crps.1), channel_id=1, replica_groups=mesh['ylo'=4,'core'=2,'z'=12,'x'=4,'yhi'=2] {'ylo','core'}, dimensions={0} | all-to-all | bytes 131072 | tf_op jit(solution)/shard_map/all_to_all | solution.py:210
  62.4 1.0 weight_term.1
  63.4 4.4 %all-to-all-start.2 = ((bf16[32,32,128]{2,1,0:T(8,128)(2,1)}), bf16[32,32,128]{2,1,0:T(8,128)(2,1)S(1)}, u32[]{:S(2)}, u32[]{:S(2)}) async-start(bf16[32,32,128]{2,1,0:T(8,128)(2,1)} %weight_term.1), calls=%async_computation.2 | async-start | bytes 524288 | tf_op jit(solution)/shard_map/all_to_all | solution.py:221
  67.8 3.1 %backward.1 = (f32[2,128,1024]{2,1,0:T(8,128)S(1)}, bf16[2,32,1024]{2,1,0:T(8,128)(2,1)S(1)}, bf16[2,32,1024]{2,1,0:T(8,128)(2,1)S(1)}) custom-call(bf16[8,2,16,128]{3,2,1,0:T(8,128)(2,1)S(1)} %all_to_all.25.grads, f32[2,256,128]{2,1,0:T(8,128)S(1)} %get-tuple-element.15.attn, bf16[2,128,1024]{2,1,0:T(8,128)(2,1)S(1)} %copy-done.1, ...), custom_call_target="tpu_custom_call" | custom-call | tf_op jit(solution)/shard_map/backward/pallas_call | solution.py:147
  70.9 8.3 %all-to-all-done.2 = bf16[32,32,128]{2,1,0:T(8,128)(2,1)S(1)} async-done(((bf16[32,32,128]{2,1,0:T(8,128)(2,1)}), bf16[32,32,128]{2,1,0:T(8,128)(2,1)S(1)}, u32[]{:S(2)}, u32[]{:S(2)}) %all-to-all-start.2) | async-done | bytes 262176 | tf_op jit(solution)/shard_map/all_to_all | solution.py:221
  79.1 0.1 reduce_sum.21
  79.2 0.7 broadcast_in_dim.4
  79.9 3.5 %all-to-all-start.3 = ((bf16[12,32,128]{2,1,0:T(8,128)(2,1)}), bf16[12,32,128]{2,1,0:T(8,128)(2,1)S(1)}, u32[]{:S(2)}, u32[]{:S(2)}) async-start(bf16[12,32,128]{2,1,0:T(8,128)(2,1)} %broadcast_in_dim.4), calls=%async_computation.3 | async-start | bytes 196608 | tf_op jit(solution)/shard_map/all_to_all | solution.py:160
  83.4 5.3 %collective-permute-start.3 = (bf16[2,32,1024]{2,1,0:T(8,128)(2,1)S(1)}, bf16[2,32,1024]{2,1,0:T(8,128)(2,1)S(1)}, u32[]{:S(2)}, u32[]{:S(2)}) collective-permute-start(bf16[2,32,1024]{2,1,0:T(8,128)(2,1)S(1)} %get-tuple-element.21), channel_id=1, source_target_pairs={{0,95},{1,0},{2,1},{3,2},{4,3},{5,4},{6,5},{7,6},{8,7},{9,8},{10,9... | collective-permute-start | bytes 393224 | tf_op jit(solution)/shard_map/ppermute | solution.py:235
  88.7 3.9 %collective-permute-start.4 = (bf16[2,32,1024]{2,1,0:T(8,128)(2,1)S(1)}, bf16[2,32,1024]{2,1,0:T(8,128)(2,1)S(1)}, u32[]{:S(2)}, u32[]{:S(2)}) collective-permute-start(bf16[2,32,1024]{2,1,0:T(8,128)(2,1)S(1)} %get-tuple-element.22), channel_id=1, source_target_pairs={{0,1},{1,2},{2,3},{3,4},{4,5},{5,6},{6,7},{7,8},{8,9},{9,10},{10,1... | collective-permute-start | bytes 393224 | tf_op jit(solution)/shard_map/ppermute | solution.py:236
  92.6 1.4 %all-to-all-done.3 = bf16[12,32,128]{2,1,0:T(8,128)(2,1)S(1)} async-done(((bf16[12,32,128]{2,1,0:T(8,128)(2,1)}), bf16[12,32,128]{2,1,0:T(8,128)(2,1)S(1)}, u32[]{:S(2)}, u32[]{:S(2)}) %all-to-all-start.3) | async-done | bytes 98336 | tf_op jit(solution)/shard_map/all_to_all | solution.py:160
  94.0 2.2 %collective-permute-start.2 = (f32[32,128]{1,0:T(8,128)S(1)}, f32[32,128]{1,0:T(8,128)S(1)}, u32[]{:S(2)}, u32[]{:S(2)}) collective-permute-start(f32[32,128]{1,0:T(8,128)S(1)} %convert_reduce_fusion), channel_id=1, source_target_pairs={{0,1},{1,0},{2,3},{3,2},{4,5},{5,4},{6,7},{7,6},{8,9},{9,8},{10,11... | collective-permute-start | bytes 49160 | tf_op jit(solution)/shard_map/ppermute | solution.py:240
  96.2 7.3 %collective-permute-done.2 = f32[32,128]{1,0:T(8,128)S(1)} collective-permute-done((f32[32,128]{1,0:T(8,128)S(1)}, f32[32,128]{1,0:T(8,128)S(1)}, u32[]{:S(2)}, u32[]{:S(2)}) %collective-permute-start.2) | collective-permute-done | bytes 16416 | tf_op jit(solution)/shard_map/ppermute | solution.py:240
  103.5 0.0 collective-permute-done.3.from_next
  103.5 0.5 collective-permute-done.4.from_prev
  104.0 0.7 broadcast_in_dim.5
  104.8 5.7 %all-to-all-start.4 = ((bf16[32,32,128]{2,1,0:T(8,128)(2,1)}), bf16[32,32,128]{2,1,0:T(8,128)(2,1)S(1)}, u32[]{:S(2)}, u32[]{:S(2)}) async-start(bf16[32,32,128]{2,1,0:T(8,128)(2,1)} %broadcast_in_dim.5), calls=%async_computation.4 | async-start | bytes 524288 | tf_op jit(solution)/shard_map/all_to_all | solution.py:160
  110.5 0.9 finish.1
  111.3 10.4 %all-to-all-done.4 = bf16[32,32,128]{2,1,0:T(8,128)(2,1)S(1)} async-done(((bf16[32,32,128]{2,1,0:T(8,128)(2,1)}), bf16[32,32,128]{2,1,0:T(8,128)(2,1)S(1)}, u32[]{:S(2)}, u32[]{:S(2)}) %all-to-all-start.4) | async-done | bytes 262176 | tf_op jit(solution)/shard_map/all_to_all | solution.py:160
  121.7 0.1 copy.14
  121.9 0.8 convert_bitcast_fusion
  (6 shorter events, 0.1 us)
Async XLA Ops:
  0.6 47.1 %copy-start = (f32[128,100]{0,1:T(8,128)S(1)}, f32[128,100]{0,1:T(8,128)}, u32[]{:S(2)}) copy-start(f32[128,100]{0,1:T(8,128)} %param.10) | copy-start | bytes 153604
  0.6 39.2 %copy-start.1 = (bf16[2,128,1024]{2,1,0:T(8,128)(2,1)S(1)}, bf16[2,128,1024]{2,1,0:T(8,128)(2,1)}, u32[]{:S(2)}) copy-start(bf16[2,128,1024]{2,1,0:T(8,128)(2,1)} %own.3) | copy-start | bytes 1572868
  0.7 39.2 %copy-start.2 = (bf16[2,128,1024]{2,1,0:T(8,128)(2,1)S(1)}, bf16[2,128,1024]{2,1,0:T(8,128)(2,1)}, u32[]{:S(2)}) copy-start(bf16[2,128,1024]{2,1,0:T(8,128)(2,1)} %queries.3) | copy-start | bytes 1572868
  1.7 25.6 %collective-permute-start.1 = (bf16[2,32,1024]{2,1,0:T(8,128)(2,1)S(1)}, bf16[2,32,1024]{2,1,0:T(8,128)(2,1)S(1)}, u32[]{:S(2)}, u32[]{:S(2)}) collective-permute-start(bf16[2,32,1024]{2,1,0:T(8,128)(2,1)S(1)} %get-tuple-element.26), channel_id=1, source_target_pairs={{0,95},{1,0},{2,1},{3,2},{4,3},{5,4},{6,5},{7,6},{8,7},{9,8},{10,9... | collective-permute-start | bytes 393224 | tf_op jit(solution)/shard_map/ppermute | solution.py:176
  24.3 15.5 %collective-permute-start = (bf16[2,32,1024]{2,1,0:T(8,128)(2,1)S(1)}, bf16[2,32,1024]{2,1,0:T(8,128)(2,1)S(1)}, u32[]{:S(2)}, u32[]{:S(2)}) collective-permute-start(bf16[2,32,1024]{2,1,0:T(8,128)(2,1)S(1)} %get-tuple-element.27), channel_id=1, source_target_pairs={{0,1},{1,2},{2,3},{3,4},{4,5},{5,6},{6,7},{7,8},{8,9},{9,10},{10,1... | collective-permute-start | bytes 393224 | tf_op jit(solution)/shard_map/ppermute | solution.py:175
  26.3 1.0 copy-start.3
  42.4 11.2 %all-to-all-start = ((f32[8,2,16,128]{3,2,1,0:T(8,128)}), f32[8,2,16,128]{3,2,1,0:T(8,128)S(1)}, u32[]{:S(2)}, u32[]{:S(2)}) async-start(f32[8,2,16,128]{3,2,1,0:T(8,128)} %get-tuple-element.14), calls=%async_computation | async-start | bytes 262144 | tf_op jit(solution)/shard_map/all_to_all | solution.py:203
  47.7 0.7 copy-start.5
  48.5 0.7 copy-start.4
  63.4 15.8 %all-to-all-start.2 = ((bf16[32,32,128]{2,1,0:T(8,128)(2,1)}), bf16[32,32,128]{2,1,0:T(8,128)(2,1)S(1)}, u32[]{:S(2)}, u32[]{:S(2)}) async-start(bf16[32,32,128]{2,1,0:T(8,128)(2,1)} %weight_term.1), calls=%async_computation.2 | async-start | bytes 524288 | tf_op jit(solution)/shard_map/all_to_all | solution.py:221
  79.9 14.1 %all-to-all-start.3 = ((bf16[12,32,128]{2,1,0:T(8,128)(2,1)}), bf16[12,32,128]{2,1,0:T(8,128)(2,1)S(1)}, u32[]{:S(2)}, u32[]{:S(2)}) async-start(bf16[12,32,128]{2,1,0:T(8,128)(2,1)} %broadcast_in_dim.4), calls=%async_computation.3 | async-start | bytes 196608 | tf_op jit(solution)/shard_map/all_to_all | solution.py:160
  83.4 20.1 %collective-permute-start.3 = (bf16[2,32,1024]{2,1,0:T(8,128)(2,1)S(1)}, bf16[2,32,1024]{2,1,0:T(8,128)(2,1)S(1)}, u32[]{:S(2)}, u32[]{:S(2)}) collective-permute-start(bf16[2,32,1024]{2,1,0:T(8,128)(2,1)S(1)} %get-tuple-element.21), channel_id=1, source_target_pairs={{0,95},{1,0},{2,1},{3,2},{4,3},{5,4},{6,5},{7,6},{8,7},{9,8},{10,9... | collective-permute-start | bytes 393224 | tf_op jit(solution)/shard_map/ppermute | solution.py:235
  88.7 15.4 %collective-permute-start.4 = (bf16[2,32,1024]{2,1,0:T(8,128)(2,1)S(1)}, bf16[2,32,1024]{2,1,0:T(8,128)(2,1)S(1)}, u32[]{:S(2)}, u32[]{:S(2)}) collective-permute-start(bf16[2,32,1024]{2,1,0:T(8,128)(2,1)S(1)} %get-tuple-element.22), channel_id=1, source_target_pairs={{0,1},{1,2},{2,3},{3,4},{4,5},{5,6},{6,7},{7,8},{8,9},{9,10},{10,1... | collective-permute-start | bytes 393224 | tf_op jit(solution)/shard_map/ppermute | solution.py:236
  94.0 9.5 %collective-permute-start.2 = (f32[32,128]{1,0:T(8,128)S(1)}, f32[32,128]{1,0:T(8,128)S(1)}, u32[]{:S(2)}, u32[]{:S(2)}) collective-permute-start(f32[32,128]{1,0:T(8,128)S(1)} %convert_reduce_fusion), channel_id=1, source_target_pairs={{0,1},{1,0},{2,3},{3,2},{4,5},{5,4},{6,7},{7,6},{8,9},{9,8},{10,11... | collective-permute-start | bytes 49160 | tf_op jit(solution)/shard_map/ppermute | solution.py:240
  104.8 17.0 %all-to-all-start.4 = ((bf16[32,32,128]{2,1,0:T(8,128)(2,1)}), bf16[32,32,128]{2,1,0:T(8,128)(2,1)S(1)}, u32[]{:S(2)}, u32[]{:S(2)}) async-start(bf16[32,32,128]{2,1,0:T(8,128)(2,1)} %broadcast_in_dim.5), calls=%async_computation.4 | async-start | bytes 524288 | tf_op jit(solution)/shard_map/all_to_all | solution.py:160

commit v2 on v1

--- a/solution.py
+++ b/solution.py
@@ -15,7 +15,7 @@
 
 MEMBER = ("ylo", "core")
 SHARD = ("z", "x", "yhi")
-SPREAD = ("x", "ylo", "core")
+SPREAD = ("x", "ylo", "yhi")
 VMEM_LIMIT = 48 * 1024 * 1024
 
 
@@ -40,9 +40,11 @@
 
 
 def forward_kernel(
-    scale, slots, own, low, high, queries, weight, attn_out, mixed_out, pred_out, window
+    scale, core, slots, own, low, high, queries, weight, attn_out, keep_out, give_out, pred_out, window
 ):
-    members, points, _ = queries.shape
+    members, points, width = queries.shape
+    half = width // 2
+    here = core[0] == 0
     rows = window.shape[0]
     nodes, reach = own.shape[1], low.shape[1]
     share = pred_out.shape[2]
@@ -65,7 +67,9 @@
             dot(attn_high, window[...], 0, 0) + dot(attn_low, window[...], 0, 0)
         )
         mixed = mixed.astype(bf16)
-        mixed_out[m] = mixed
+        left, right = mixed[:, :half], mixed[:, half:]
+        keep_out[m] = jnp.where(here, left, right)
+        give_out[m] = jnp.where(here, right, left)
         pred = dot(mixed, weight[...], 1, 1)
         for k in range(points // share):
             pred_out[k, m] = pred[k * share : (k + 1) * share]
@@ -87,17 +91,22 @@
         grad = weighting[...] * (
             skill / count - (1.0 - eps_fair) / (count * (count - 1)) * spread[k]
         )
-        out[k // each, k % each] = grad.astype(bf16)
-
-
-def weight_kernel(grads, mixed, out):
-    owners, members, share, lanes = grads.shape
+        grad = grad.astype(bf16)
+        group, m = k // each, k % each
+        out[group, m] = grad
+        out[group ^ 1, each + m] = grad
+
+
+def weight_kernel(grads, keep, got, out):
+    owners, _, share, lanes = grads.shape
+    members = keep.shape[0]
     points = owners * share
     total = None
     for m in range(members):
-        g = grads[:, m].reshape(points, lanes)
-        term = dot(g, mixed[m], 0, 0)
-        total = term if total is None else total + term
+        for part, mixed in ((m, keep), (members + m, got)):
+            g = grads[:, part].reshape(points, lanes)
+            term = dot(g, mixed[m], 0, 0)
+            total = term if total is None else total + term
     pieces, high, wide = out.shape
     across = total.shape[1] // wide
     for k in range(pieces):
@@ -105,10 +114,34 @@
         out[k] = total[r : r + high, c : c + wide].astype(bf16)
 
 
+def add_kernel(terms, out):
+    total = terms[0].astype(f32)
+    for k in range(1, terms.shape[0]):
+        total = total + terms[k].astype(f32)
+    total = total.astype(bf16)
+    for k in range(out.shape[0]):
+        out[k] = total
+
+
+def assemble_kernel(core, mine, other, out):
+    pieces, high, wide = mine.shape
+    half = out.shape[1] // 2
+    across = half // wide
+    here = core[0] == 0
+    for k in range(pieces):
+        r, c = k // across * high, k % across * wide
+        size = min(high, out.shape[0] - r)
+        if size > 0:
+            a, b = mine[k].astype(f32)[:size], other[k].astype(f32)[:size]
+            out[r : r + size, c : c + wide] = jnp.where(here, a, b)
+            out[r : r + size, half + c : half + c + wide] = jnp.where(here, b, a)
+
+
 def backward_kernel(
     scale, grads, attn, own, low, high, queries, weight, own_out, low_out, high_out, window
 ):
-    owners, members, share, lanes = grads.shape
+    owners, _, share, lanes = grads.shape
+    members = queries.shape[0]
     points = owners * share
     rows = window.shape[0]
     nodes, reach = own.shape[1], low.shape[1]
@@ -141,13 +174,13 @@
         out[m, nodes - reach :] = (own[m, nodes - reach :] + from_next[m].astype(f32)).astype(bf16)
 
 
-def call(kernel, out_shape, args, scratch=(), name=None):
-    vmem = pl.BlockSpec(memory_space=pltpu.VMEM)
+def call(kernel, out_shape, args, scratch=(), name=None, scalars=0):
+    vmem, smem = pl.BlockSpec(memory_space=pltpu.VMEM), pl.BlockSpec(memory_space=pltpu.SMEM)
     single = not isinstance(out_shape, (list, tuple))
     return pl.pallas_call(
         kernel,
         out_shape=out_shape,
-        in_specs=[vmem] * len(args),
+        in_specs=[smem] * scalars + [vmem] * (len(args) - scalars),
         out_specs=vmem if single else [vmem] * len(out_shape),
         scratch_shapes=list(scratch),
         compiler_params=pltpu.CompilerParams(vmem_limit_bytes=VMEM_LIMIT),
@@ -155,9 +188,12 @@
     )(*args)
 
 
-def spread_out(x, axes):
-    count = lax.axis_size(axes)
-    return lax.all_to_all(jnp.broadcast_to(x[None], (count,) + x.shape), axes, 0, 0, tiled=True)
+def add_up(terms, copies, name):
+    return call(add_kernel, jax.ShapeDtypeStruct((copies,) + terms.shape[1:], bf16), (terms,), name=name)
+
+
+def exchange(x, axes):
+    return lax.all_to_all(x, axes, 0, 0, tiled=True)
 
 
 def local(latents, queries, neighbours, truth, area_weight, var_weight, proj_weight):
@@ -189,36 +225,40 @@
 
     window_rows = 2 * LANES
     window = pltpu.VMEM((window_rows, width), bf16)
-    attn, mixed, pred = call(
+    core = lax.axis_index("core").astype(jnp.int32).reshape(1)
+    swap = [(0, 1), (1, 0)]
+    attn, keep, give, pred = call(
         functools.partial(forward_kernel, scale),
         [
             jax.ShapeDtypeStruct((members, window_rows, points), f32),
-            jax.ShapeDtypeStruct((members, points, width), bf16),
+            jax.ShapeDtypeStruct((members, points, width // 2), bf16),
+            jax.ShapeDtypeStruct((members, points, width // 2), bf16),
             jax.ShapeDtypeStruct((owners, members, share, LANES), f32),
         ],
-        (slots, latents, low, high, queries, weight),
+        (core, slots, latents, low, high, queries, weight),
         [window],
         name="forward",
-    )
-    rows = lax.all_to_all(pred, MEMBER, 0, 0, tiled=True)
+        scalars=1,
+    )
+    rows = exchange(pred, MEMBER)
+    got = lax.ppermute(give, "core", swap)
     owner_grad = call(
         crps_kernel,
-        jax.ShapeDtypeStruct(rows.shape, bf16),
+        jax.ShapeDtypeStruct((owners, 2 * members, share, LANES), bf16),
         (rows, target, weighting),
         name="crps",
     )
-    grads = lax.all_to_all(owner_grad, MEMBER, 0, 0, tiled=True)
-
-    across = width // LANES
+    grads = exchange(owner_grad, MEMBER)
+
     pieces = lax.axis_size(SPREAD)
-    tall = LANES // (pieces // across)
+    tall = width // 2 // pieces
     term = call(
         weight_kernel,
         jax.ShapeDtypeStruct((pieces, tall, LANES), bf16),
-        (grads, mixed),
+        (grads, keep, got),
         name="weight_term",
     )
-    term = lax.all_to_all(term, SPREAD, 0, 0, tiled=True)
+    term = exchange(term, SPREAD)
 
     own_part, low_part, high_part = call(
         functools.partial(backward_kernel, scale),
@@ -234,14 +274,16 @@
     term, low_part, high_part = lax.optimization_barrier((term, low_part, high_part))
     from_next = lax.ppermute(low_part, SHARD, backward)
     from_prev = lax.ppermute(high_part, SHARD, forward)
-
-    piece = jnp.sum(term.astype(f32), axis=0).astype(bf16)
-    piece = jnp.sum(spread_out(piece, "z").astype(f32), axis=0)
-    piece = piece + lax.ppermute(piece, "yhi", [(0, 1), (1, 0)])
-    piece, from_next, from_prev = lax.optimization_barrier((piece, from_next, from_prev))
-    full = spread_out(piece.astype(bf16), SPREAD).astype(f32)
-    full = full.reshape(pieces // across, across, tall, LANES).transpose(0, 2, 1, 3)
-    proj_grad = full.reshape(LANES, width)[:variables].T
+    piece = exchange(add_up(term, lax.axis_size("z"), "add_plane"), "z")
+    mine = exchange(add_up(piece, pieces, "add_z"), SPREAD)
+    other = lax.ppermute(mine, "core", swap)
+    proj_grad = call(
+        assemble_kernel,
+        jax.ShapeDtypeStruct((variables, width), f32),
+        (core, mine, other),
+        name="assemble",
+        scalars=1,
+    ).T
 
     latent_grad = call(
         finish_kernel,

time: 123 us -> 121 us (0.984)
  the two profiles are of different devices: /device:TPU:1 before, /device:TPU:2 now
where the time goes in v2:
time: 121 us; the launch traced here: 120 us
  starting transfers between devices  57.2 us (47%)
  waiting for transfers between devices  35.6 us (29%)
  blocking collectives  13.5 us (11%)
  Pallas kernels  9.87 us (8%)
  local copies, waits for them, and re-layouts  2.97 us (2%)
    all_to_all x4, starting transfers between devices, exchange(): return lax.all_to_all(x, axes, 0, 0, tiled=True)  32.5 us
    all_to_all x4, waiting for transfers between devices, exchange(): return lax.all_to_all(x, axes, 0, 0, tiled=True)  19 us
    all_to_all x1, blocking collectives, exchange(): return lax.all_to_all(x, axes, 0, 0, tiled=True)  13.5 us
    pallas_call x8, Pallas kernels, call(): pl.pallas_call(kernel, out_shape=out_shape, in_specs=[smem] * scalars + [...  9.87 us
    ppermute x1, waiting for transfers between devices, local(): low = lax.ppermute(latents[:, nodes - reach:], SHARD, forward)  7.8 us
    ppermute x1, starting transfers between devices, local(): high = lax.ppermute(latents[:, :reach], SHARD, backward)  7.7 us
    ppermute x1, starting transfers between devices, local(): from_prev = lax.ppermute(high_part, SHARD, forward)  7.29 us
    ppermute x1, waiting for transfers between devices, local(): from_next = lax.ppermute(low_part, SHARD, backward)  6.11 us
  transfers between devices with their start and end apart: 10, of which 7 were waited for; matrix products, arithmetic and copies ran while one was open for 2% of the time, Pallas kernels for 4%

profile of v2, /device:TPU:2, one launch (start us, length us, event | category | flops | bytes accessed | tf_op | source)
XLA Modules:
  0.0 120.0 jit_solution(2812510997384712108)
XLA Ops:
  0.6 0.0 copy-start
  0.6 0.0 copy-start.1
  0.7 0.0 copy-start.2
  0.7 1.1 fusion.2
  1.7 7.7 %collective-permute-start.1 = (bf16[2,32,1024]{2,1,0:T(8,128)(2,1)S(1)}, bf16[2,32,1024]{2,1,0:T(8,128)(2,1)S(1)}, u32[]{:S(2)}, u32[]{:S(2)}) collective-permute-start(bf16[2,32,1024]{2,1,0:T(8,128)(2,1)S(1)} %get-tuple-element.22), channel_id=1, source_target_pairs={{0,95},{1,0},{2,1},{3,2},{4,3},{5,4},{6,5},{7,6},{8,7},{9,8},{10,9... | collective-permute-start | bytes 393224 | tf_op jit(solution)/shard_map/ppermute | solution.py:212
  9.5 2.0 %collective-permute-start = (bf16[2,32,1024]{2,1,0:T(8,128)(2,1)S(1)}, bf16[2,32,1024]{2,1,0:T(8,128)(2,1)S(1)}, u32[]{:S(2)}, u32[]{:S(2)}) collective-permute-start(bf16[2,32,1024]{2,1,0:T(8,128)(2,1)S(1)} %get-tuple-element.23), channel_id=1, source_target_pairs={{0,1},{1,2},{2,3},{3,4},{4,5},{5,6},{6,7},{7,8},{8,9},{9,10},{10,1... | collective-permute-start | bytes 393224 | tf_op jit(solution)/shard_map/ppermute | solution.py:211
  11.5 0.7 dynamic_slice.7
  12.3 0.0 copy-start.3
  12.3 1.0 pad.11.weight
  13.2 0.0 copy-done.3
  13.3 2.7 %collective-permute-done.1.high = bf16[2,32,1024]{2,1,0:T(8,128)(2,1)S(1)} collective-permute-done((bf16[2,32,1024]{2,1,0:T(8,128)(2,1)S(1)}, bf16[2,32,1024]{2,1,0:T(8,128)(2,1)S(1)}, u32[]{:S(2)}, u32[]{:S(2)}) %collective-permute-start.1) | collective-permute-done | bytes 131104 | tf_op jit(solution)/shard_map/ppermute | solution.py:212
  16.0 7.8 %collective-permute-done.low = bf16[2,32,1024]{2,1,0:T(8,128)(2,1)S(1)} collective-permute-done((bf16[2,32,1024]{2,1,0:T(8,128)(2,1)S(1)}, bf16[2,32,1024]{2,1,0:T(8,128)(2,1)S(1)}, u32[]{:S(2)}, u32[]{:S(2)}) %collective-permute-start) | collective-permute-done | bytes 131104 | tf_op jit(solution)/shard_map/ppermute | solution.py:211
  23.8 0.0 copy-done.1
  23.8 0.0 copy-done.2
  23.8 2.5 %forward.1 = (f32[2,256,128]{2,1,0:T(8,128)S(1)}, bf16[2,128,512]{2,1,0:T(8,128)(2,1)S(1)}, bf16[2,128,512]{2,1,0:T(8,128)(2,1)S(1)}, f32[8,2,16,128]{3,2,1,0:T(8,128)}) custom-call(s32[1]{0:T(128)} %bitcast.core, s32[4,128]{1,0:T(4,128)S(1)} %fusion.slots, bf16[2,128,1024]{2,1,0:T(8,128)(2,1)S(1)} %copy-done.1, ...), custom_call_target="tpu_custom_call" | custom-call | tf_op jit(solution)/shard_map/forward/pallas_call | solution.py:180
  26.3 0.0 copy-start.4
  26.3 3.8 %all-to-all-start = ((f32[8,2,16,128]{3,2,1,0:T(8,128)}), f32[8,2,16,128]{3,2,1,0:T(8,128)S(1)}, u32[]{:S(2)}, u32[]{:S(2)}) async-start(f32[8,2,16,128]{3,2,1,0:T(8,128)} %get-tuple-element.12), calls=%async_computation | async-start | bytes 262144 | tf_op jit(solution)/shard_map/all_to_all | solution.py:196
  30.0 0.0 copy-done.4
  30.1 0.1 broadcast_multiply_fusion
  30.1 2.4 %collective-permute-start.2 = (bf16[2,128,512]{2,1,0:T(8,128)(2,1)S(1)}, bf16[2,128,512]{2,1,0:T(8,128)(2,1)S(1)}, u32[]{:S(2)}, u32[]{:S(2)}) collective-permute-start(bf16[2,128,512]{2,1,0:T(8,128)(2,1)S(1)} %get-tuple-element.16), channel_id=1, source_target_pairs={{0,96},{96,0},{1,97},{97,1},{2,98},{98,2},{3,99},{99,3},{4,100},{1... | collective-permute-start | bytes 786440 | tf_op jit(solution)/shard_map/ppermute | solution.py:244
  32.5 0.0 copy-done
  32.5 0.1 constant_dynamic-slice_fusion
  32.6 0.1 copy.10
  32.7 4.1 %all-to-all-done.rows = f32[8,2,16,128]{3,2,1,0:T(8,128)S(1)} async-done(((f32[8,2,16,128]{3,2,1,0:T(8,128)}), f32[8,2,16,128]{3,2,1,0:T(8,128)S(1)}, u32[]{:S(2)}, u32[]{:S(2)}) %all-to-all-start) | async-done | bytes 131104 | tf_op jit(solution)/shard_map/all_to_all | solution.py:196
  36.8 0.9 crps.1
  37.8 3.4 %all-to-all-start.1 = ((bf16[8,4,16,128]{3,2,1,0:T(8,128)(2,1)}), bf16[8,4,16,128]{3,2,1,0:T(8,128)(2,1)S(1)}, u32[]{:S(2)}, u32[]{:S(2)}) async-start(bf16[8,4,16,128]{3,2,1,0:T(8,128)(2,1)} %crps.1), calls=%async_computation.1 | async-start | bytes 262144 | tf_op jit(solution)/shard_map/all_to_all | solution.py:196
  41.1 0.0 collective-permute-done.2.got
  41.2 6.7 %all-to-all-done.1.grads = bf16[8,4,16,128]{3,2,1,0:T(8,128)(2,1)S(1)} async-done(((bf16[8,4,16,128]{3,2,1,0:T(8,128)(2,1)}), bf16[8,4,16,128]{3,2,1,0:T(8,128)(2,1)S(1)}, u32[]{:S(2)}, u32[]{:S(2)}) %all-to-all-start.1) | async-done | bytes 131104 | tf_op jit(solution)/shard_map/all_to_all | solution.py:196
  47.9 1.0 weight_term.1
  48.8 20.4 %all-to-all-start.2 = ((bf16[32,16,128]{2,1,0:T(8,128)(2,1)}), bf16[32,16,128]{2,1,0:T(8,128)(2,1)S(1)}, u32[]{:S(2)}, u32[]{:S(2)}) async-start(bf16[32,16,128]{2,1,0:T(8,128)(2,1)} %weight_term.1), calls=%async_computation.2 | async-start | bytes 262144 | tf_op jit(solution)/shard_map/all_to_all | solution.py:196
  69.2 3.1 %backward.1 = (f32[2,128,1024]{2,1,0:T(8,128)S(1)}, bf16[2,32,1024]{2,1,0:T(8,128)(2,1)S(1)}, bf16[2,32,1024]{2,1,0:T(8,128)(2,1)S(1)}) custom-call(bf16[8,4,16,128]{3,2,1,0:T(8,128)(2,1)S(1)} %all-to-all-done.1.grads, f32[2,256,128]{2,1,0:T(8,128)S(1)} %get-tuple-element.13.attn, bf16[2,128,1024]{2,1,0:T(8,128)(2,1)S(1)} %copy-done.1, ...), custom_call_target="tpu_custom_call" | custom-call | tf_op jit(solution)/shard_map/backward/pallas_call | solution.py:180
  72.3 6.3 %all-to-all-done.2.terms = bf16[32,16,128]{2,1,0:T(8,128)(2,1)S(1)} async-done(((bf16[32,16,128]{2,1,0:T(8,128)(2,1)}), bf16[32,16,128]{2,1,0:T(8,128)(2,1)S(1)}, u32[]{:S(2)}, u32[]{:S(2)}) %all-to-all-start.2) | async-done | bytes 131104 | tf_op jit(solution)/shard_map/all_to_all | solution.py:196
  78.7 13.5 %all_to_all.25.terms = bf16[12,16,128]{2,1,0:T(8,128)(2,1)S(1)} all-to-all(bf16[12,16,128]{2,1,0:T(8,128)(2,1)S(1)} %add_plane.1), channel_id=1, replica_groups=mesh['ylo'=4,'core'=2,'z'=12,'x'=4,'yhi'=2] {'z'}, dimensions={0} | all-to-all | bytes 98304 | tf_op jit(solution)/shard_map/all_to_all | solution.py:196
  92.2 0.7 add_z.1
  92.9 5.0 %all-to-all-start.4 = ((bf16[32,16,128]{2,1,0:T(8,128)(2,1)}), bf16[32,16,128]{2,1,0:T(8,128)(2,1)S(1)}, u32[]{:S(2)}, u32[]{:S(2)}) async-start(bf16[32,16,128]{2,1,0:T(8,128)(2,1)} %add_z.1), calls=%async_computation.4 | async-start | bytes 262144 | tf_op jit(solution)/shard_map/all_to_all | solution.py:196
  97.9 7.3 %collective-permute-start.3 = (bf16[2,32,1024]{2,1,0:T(8,128)(2,1)S(1)}, bf16[2,32,1024]{2,1,0:T(8,128)(2,1)S(1)}, u32[]{:S(2)}, u32[]{:S(2)}) collective-permute-start(bf16[2,32,1024]{2,1,0:T(8,128)(2,1)S(1)} %get-tuple-element.19), channel_id=1, source_target_pairs={{0,1},{1,2},{2,3},{3,4},{4,5},{5,6},{6,7},{7,8},{8,9},{9,10},{10,1... | collective-permute-start | bytes 393224 | tf_op jit(solution)/shard_map/ppermute | solution.py:276
  105.1 3.4 %collective-permute-start.4 = (bf16[2,32,1024]{2,1,0:T(8,128)(2,1)S(1)}, bf16[2,32,1024]{2,1,0:T(8,128)(2,1)S(1)}, u32[]{:S(2)}, u32[]{:S(2)}) collective-permute-start(bf16[2,32,1024]{2,1,0:T(8,128)(2,1)S(1)} %get-tuple-element.20), channel_id=1, source_target_pairs={{0,95},{1,0},{2,1},{3,2},{4,3},{5,4},{6,5},{7,6},{8,7},{9,8},{10,9... | collective-permute-start | bytes 393224 | tf_op jit(solution)/shard_map/ppermute | solution.py:275
  108.5 1.8 %all-to-all-done.4.mine = bf16[32,16,128]{2,1,0:T(8,128)(2,1)S(1)} async-done(((bf16[32,16,128]{2,1,0:T(8,128)(2,1)}), bf16[32,16,128]{2,1,0:T(8,128)(2,1)S(1)}, u32[]{:S(2)}, u32[]{:S(2)}) %all-to-all-start.4) | async-done | bytes 131104 | tf_op jit(solution)/shard_map/all_to_all | solution.py:196
  110.4 1.9 %collective-permute-start.5 = (bf16[32,16,128]{2,1,0:T(8,128)(2,1)S(1)}, bf16[32,16,128]{2,1,0:T(8,128)(2,1)S(1)}, u32[]{:S(2)}, u32[]{:S(2)}) collective-permute-start(bf16[32,16,128]{2,1,0:T(8,128)(2,1)S(1)} %all-to-all-done.4.mine), channel_id=1, source_target_pairs={{0,96},{96,0},{1,97},{97,1},{2,98},{98,2},{3,99},{99,3},{4,100},{1... | collective-permute-start | bytes 393224 | tf_op jit(solution)/shard_map/ppermute | solution.py:279
  112.3 0.0 collective-permute-done.3.from_prev
  112.3 6.1 %collective-permute-done.4.from_next = bf16[2,32,1024]{2,1,0:T(8,128)(2,1)S(1)} collective-permute-done((bf16[2,32,1024]{2,1,0:T(8,128)(2,1)S(1)}, bf16[2,32,1024]{2,1,0:T(8,128)(2,1)S(1)}, u32[]{:S(2)}, u32[]{:S(2)}) %collective-permute-start.4) | collective-permute-done | bytes 131104 | tf_op jit(solution)/shard_map/ppermute | solution.py:275
  118.4 0.9 finish.1
  119.3 0.0 collective-permute-done.5.other
  119.3 0.8 assemble.1
  (4 shorter events, 0.1 us)
Async XLA Ops:
  0.6 31.9 %copy-start = (f32[128,100]{0,1:T(8,128)S(1)}, f32[128,100]{0,1:T(8,128)}, u32[]{:S(2)}) copy-start(f32[128,100]{0,1:T(8,128)} %param.10) | copy-start | bytes 153604
  0.6 23.1 %copy-start.1 = (bf16[2,128,1024]{2,1,0:T(8,128)(2,1)S(1)}, bf16[2,128,1024]{2,1,0:T(8,128)(2,1)}, u32[]{:S(2)}) copy-start(bf16[2,128,1024]{2,1,0:T(8,128)(2,1)} %own.3) | copy-start | bytes 1572868
  0.7 23.1 %copy-start.2 = (bf16[2,128,1024]{2,1,0:T(8,128)(2,1)S(1)}, bf16[2,128,1024]{2,1,0:T(8,128)(2,1)}, u32[]{:S(2)}) copy-start(bf16[2,128,1024]{2,1,0:T(8,128)(2,1)} %queries.3) | copy-start | bytes 1572868
  1.7 14.2 %collective-permute-start.1 = (bf16[2,32,1024]{2,1,0:T(8,128)(2,1)S(1)}, bf16[2,32,1024]{2,1,0:T(8,128)(2,1)S(1)}, u32[]{:S(2)}, u32[]{:S(2)}) collective-permute-start(bf16[2,32,1024]{2,1,0:T(8,128)(2,1)S(1)} %get-tuple-element.22), channel_id=1, source_target_pairs={{0,95},{1,0},{2,1},{3,2},{4,3},{5,4},{6,5},{7,6},{8,7},{9,8},{10,9... | collective-permute-start | bytes 393224 | tf_op jit(solution)/shard_map/ppermute | solution.py:212
  9.5 14.3 %collective-permute-start = (bf16[2,32,1024]{2,1,0:T(8,128)(2,1)S(1)}, bf16[2,32,1024]{2,1,0:T(8,128)(2,1)S(1)}, u32[]{:S(2)}, u32[]{:S(2)}) collective-permute-start(bf16[2,32,1024]{2,1,0:T(8,128)(2,1)S(1)} %get-tuple-element.23), channel_id=1, source_target_pairs={{0,1},{1,2},{2,3},{3,4},{4,5},{5,6},{6,7},{7,8},{8,9},{9,10},{10,1... | collective-permute-start | bytes 393224 | tf_op jit(solution)/shard_map/ppermute | solution.py:211
  12.3 1.0 copy-start.3
  26.3 3.8 %copy-start.4 = (f32[100]{0:T(128)S(1)}, f32[100]{0:T(128)}, u32[]{:S(2)}) copy-start(f32[100]{0:T(128)} %param.12) | copy-start | bytes 1204
  26.3 10.6 %all-to-all-start = ((f32[8,2,16,128]{3,2,1,0:T(8,128)}), f32[8,2,16,128]{3,2,1,0:T(8,128)S(1)}, u32[]{:S(2)}, u32[]{:S(2)}) async-start(f32[8,2,16,128]{3,2,1,0:T(8,128)} %get-tuple-element.12), calls=%async_computation | async-start | bytes 262144 | tf_op jit(solution)/shard_map/all_to_all | solution.py:196
  30.1 11.0 %collective-permute-start.2 = (bf16[2,128,512]{2,1,0:T(8,128)(2,1)S(1)}, bf16[2,128,512]{2,1,0:T(8,128)(2,1)S(1)}, u32[]{:S(2)}, u32[]{:S(2)}) collective-permute-start(bf16[2,128,512]{2,1,0:T(8,128)(2,1)S(1)} %get-tuple-element.16), channel_id=1, source_target_pairs={{0,96},{96,0},{1,97},{97,1},{2,98},{98,2},{3,99},{99,3},{4,100},{1... | collective-permute-start | bytes 786440 | tf_op jit(solution)/shard_map/ppermute | solution.py:244
  37.8 10.1 %all-to-all-start.1 = ((bf16[8,4,16,128]{3,2,1,0:T(8,128)(2,1)}), bf16[8,4,16,128]{3,2,1,0:T(8,128)(2,1)S(1)}, u32[]{:S(2)}, u32[]{:S(2)}) async-start(bf16[8,4,16,128]{3,2,1,0:T(8,128)(2,1)} %crps.1), calls=%async_computation.1 | async-start | bytes 262144 | tf_op jit(solution)/shard_map/all_to_all | solution.py:196
  48.8 29.8 %all-to-all-start.2 = ((bf16[32,16,128]{2,1,0:T(8,128)(2,1)}), bf16[32,16,128]{2,1,0:T(8,128)(2,1)S(1)}, u32[]{:S(2)}, u32[]{:S(2)}) async-start(bf16[32,16,128]{2,1,0:T(8,128)(2,1)} %weight_term.1), calls=%async_computation.2 | async-start | bytes 262144 | tf_op jit(solution)/shard_map/all_to_all | solution.py:196
  92.9 17.5 %all-to-all-start.4 = ((bf16[32,16,128]{2,1,0:T(8,128)(2,1)}), bf16[32,16,128]{2,1,0:T(8,128)(2,1)S(1)}, u32[]{:S(2)}, u32[]{:S(2)}) async-start(bf16[32,16,128]{2,1,0:T(8,128)(2,1)} %add_z.1), calls=%async_computation.4 | async-start | bytes 262144 | tf_op jit(solution)/shard_map/all_to_all | solution.py:196
  97.9 14.4 %collective-permute-start.3 = (bf16[2,32,1024]{2,1,0:T(8,128)(2,1)S(1)}, bf16[2,32,1024]{2,1,0:T(8,128)(2,1)S(1)}, u32[]{:S(2)}, u32[]{:S(2)}) collective-permute-start(bf16[2,32,1024]{2,1,0:T(8,128)(2,1)S(1)} %get-tuple-element.19), channel_id=1, source_target_pairs={{0,1},{1,2},{2,3},{3,4},{4,5},{5,6},{6,7},{7,8},{8,9},{9,10},{10,1... | collective-permute-start | bytes 393224 | tf_op jit(solution)/shard_map/ppermute | solution.py:276
  105.1 13.2 %collective-permute-start.4 = (bf16[2,32,1024]{2,1,0:T(8,128)(2,1)S(1)}, bf16[2,32,1024]{2,1,0:T(8,128)(2,1)S(1)}, u32[]{:S(2)}, u32[]{:S(2)}) collective-permute-start(bf16[2,32,1024]{2,1,0:T(8,128)(2,1)S(1)} %get-tuple-element.20), channel_id=1, source_target_pairs={{0,95},{1,0},{2,1},{3,2},{4,3},{5,4},{6,5},{7,6},{8,7},{9,8},{10,9... | collective-permute-start | bytes 393224 | tf_op jit(solution)/shard_map/ppermute | solution.py:275
  110.4 8.9 %collective-permute-start.5 = (bf16[32,16,128]{2,1,0:T(8,128)(2,1)S(1)}, bf16[32,16,128]{2,1,0:T(8,128)(2,1)S(1)}, u32[]{:S(2)}, u32[]{:S(2)}) collective-permute-start(bf16[32,16,128]{2,1,0:T(8,128)(2,1)S(1)} %all-to-all-done.4.mine), channel_id=1, source_target_pairs={{0,96},{96,0},{1,97},{97,1},{2,98},{98,2},{3,99},{99,3},{4,100},{1... | collective-permute-start | bytes 393224 | tf_op jit(solution)/shard_map/ppermute | solution.py:279

commit v3 on v2

--- a/solution.py
+++ b/solution.py
@@ -196,6 +196,16 @@
     return lax.all_to_all(x, axes, 0, 0, tiled=True)
 
 
+def whole_exchange(x):
+    return exchange(x, SPREAD)
+
+
+def split_exchange(x):
+    x = x.reshape((lax.axis_size(SPREAD[0]), -1) + x.shape[1:])
+    x = exchange(x, SPREAD[:1])
+    return lax.all_to_all(x, SPREAD[1:], 1, 1, tiled=True).reshape((-1,) + x.shape[2:])
+
+
 def local(latents, queries, neighbours, truth, area_weight, var_weight, proj_weight):
     members, nodes, width = latents.shape
     points = queries.shape[1]
@@ -275,7 +285,7 @@
     from_next = lax.ppermute(low_part, SHARD, backward)
     from_prev = lax.ppermute(high_part, SHARD, forward)
     piece = exchange(add_up(term, lax.axis_size("z"), "add_plane"), "z")
-    mine = exchange(add_up(piece, pieces, "add_z"), SPREAD)
+    mine = lax.cond(var_weight[0] > 0.0, whole_exchange, split_exchange, add_up(piece, pieces, "add_z"))
     other = lax.ppermute(mine, "core", swap)
     proj_grad = call(
         assemble_kernel,

time: 121 us -> 117 us (0.967)
  the two profiles are of different devices: /device:TPU:2 before, /device:TPU:1 now
where the time goes in v3:
time: 117 us; the launch traced here: 116 us
  starting transfers between devices  73.3 us (63%)
  waiting for transfers between devices  16.9 us (14%)
  blocking collectives  12.3 us (11%)
  Pallas kernels  9.84 us (8%)
  local copies, waits for them, and re-layouts  2.97 us (3%)
    all_to_all x4, starting transfers between devices, exchange(): return lax.all_to_all(x, axes, 0, 0, tiled=True)  26.9 us
    ppermute x1, starting transfers between devices, local(): high = lax.ppermute(latents[:, :reach], SHARD, backward)  16.2 us
    all_to_all x4, waiting for transfers between devices, exchange(): return lax.all_to_all(x, axes, 0, 0, tiled=True)  15.6 us
    all_to_all x1, blocking collectives, exchange(): return lax.all_to_all(x, axes, 0, 0, tiled=True)  12.3 us
    ppermute x1, starting transfers between devices, local(): from_next = lax.ppermute(low_part, SHARD, backward)  10.4 us
    pallas_call x8, Pallas kernels, call(): pl.pallas_call(kernel, out_shape=out_shape, in_specs=[smem] * scalars + [...  9.84 us
    ppermute x1, starting transfers between devices, local(): low = lax.ppermute(latents[:, nodes - reach:], SHARD, forward)  8.28 us
    ppermute x1, starting transfers between devices, local(): other = lax.ppermute(mine, 'core', swap)  6.46 us
  transfers between devices with their start and end apart: 10, of which 5 were waited for; matrix products, arithmetic and copies ran while one was open for 2% of the time, Pallas kernels for 4%

profile of v3, /device:TPU:1, one launch (start us, length us, event | category | flops | bytes accessed | tf_op | source)
XLA Modules:
  0.0 116.2 jit_solution(15768700994058640802)
XLA Ops:
  0.6 0.0 copy-start
  0.6 0.0 copy-start.1
  0.7 0.0 copy-start.2
  0.7 1.1 fusion.2
  1.7 8.3 %collective-permute-start = (bf16[2,32,1024]{2,1,0:T(8,128)(2,1)S(1)}, bf16[2,32,1024]{2,1,0:T(8,128)(2,1)S(1)}, u32[]{:S(2)}, u32[]{:S(2)}) collective-permute-start(bf16[2,32,1024]{2,1,0:T(8,128)(2,1)S(1)} %get-tuple-element.28), channel_id=1, source_target_pairs={{0,1},{1,2},{2,3},{3,4},{4,5},{5,6},{6,7},{7,8},{8,9},{9,10},{10,1... | collective-permute-start | bytes 393224 | tf_op jit(solution)/shard_map/ppermute | solution.py:221
  10.0 16.2 %collective-permute-start.1 = (bf16[2,32,1024]{2,1,0:T(8,128)(2,1)S(1)}, bf16[2,32,1024]{2,1,0:T(8,128)(2,1)S(1)}, u32[]{:S(2)}, u32[]{:S(2)}) collective-permute-start(bf16[2,32,1024]{2,1,0:T(8,128)(2,1)S(1)} %get-tuple-element.27), channel_id=1, source_target_pairs={{0,95},{1,0},{2,1},{3,2},{4,3},{5,4},{6,5},{7,6},{8,7},{9,8},{10,9... | collective-permute-start | bytes 393224 | tf_op jit(solution)/shard_map/ppermute | solution.py:222
  26.3 0.7 dynamic_slice.7
  27.0 0.0 copy-start.3
  27.0 1.0 pad.11.weight
  28.0 0.0 copy-done.3
  28.0 1.1 collective-permute-done.low
  29.2 0.0 collective-permute-done.1.high
  29.2 0.0 copy-done.1
  29.2 0.0 copy-done.2
  29.2 2.5 %forward.1 = (f32[2,256,128]{2,1,0:T(8,128)S(1)}, bf16[2,128,512]{2,1,0:T(8,128)(2,1)S(1)}, bf16[2,128,512]{2,1,0:T(8,128)(2,1)S(1)}, f32[8,2,16,128]{3,2,1,0:T(8,128)}) custom-call(s32[1]{0:T(128)} %bitcast.2.core, s32[4,128]{1,0:T(4,128)S(1)} %fusion.slots, bf16[2,128,1024]{2,1,0:T(8,128)(2,1)S(1)} %copy-done.1, ...), custom_call_target="tpu_custom_call" | custom-call | tf_op jit(solution)/shard_map/forward/pallas_call | solution.py:180
  31.7 0.0 copy-start.4
  31.7 5.6 %all-to-all-start.3 = ((f32[8,2,16,128]{3,2,1,0:T(8,128)}), f32[8,2,16,128]{3,2,1,0:T(8,128)S(1)}, u32[]{:S(2)}, u32[]{:S(2)}) async-start(f32[8,2,16,128]{3,2,1,0:T(8,128)} %get-tuple-element.17), calls=%async_computation.3 | async-start | bytes 262144 | tf_op jit(solution)/shard_map/all_to_all | solution.py:196
  37.2 0.0 copy-done.4
  37.3 0.1 broadcast_multiply_fusion
  37.3 2.0 %collective-permute-start.2 = (bf16[2,128,512]{2,1,0:T(8,128)(2,1)S(1)}, bf16[2,128,512]{2,1,0:T(8,128)(2,1)S(1)}, u32[]{:S(2)}, u32[]{:S(2)}) collective-permute-start(bf16[2,128,512]{2,1,0:T(8,128)(2,1)S(1)} %get-tuple-element.21), channel_id=1, source_target_pairs={{0,96},{96,0},{1,97},{97,1},{2,98},{98,2},{3,99},{99,3},{4,100},{1... | collective-permute-start | bytes 786440 | tf_op jit(solution)/shard_map/ppermute | solution.py:254
  39.3 0.0 copy-done
  39.4 0.1 constant_dynamic-slice_fusion
  39.4 0.1 copy.14
  39.5 3.6 %all-to-all-done.3.rows = f32[8,2,16,128]{3,2,1,0:T(8,128)S(1)} async-done(((f32[8,2,16,128]{3,2,1,0:T(8,128)}), f32[8,2,16,128]{3,2,1,0:T(8,128)S(1)}, u32[]{:S(2)}, u32[]{:S(2)}) %all-to-all-start.3) | async-done | bytes 131104 | tf_op jit(solution)/shard_map/all_to_all | solution.py:196
  43.1 0.9 crps.1
  44.0 4.2 %all-to-all-start.4 = ((bf16[8,4,16,128]{3,2,1,0:T(8,128)(2,1)}), bf16[8,4,16,128]{3,2,1,0:T(8,128)(2,1)S(1)}, u32[]{:S(2)}, u32[]{:S(2)}) async-start(bf16[8,4,16,128]{3,2,1,0:T(8,128)(2,1)} %crps.1), calls=%async_computation.4 | async-start | bytes 262144 | tf_op jit(solution)/shard_map/all_to_all | solution.py:196
  48.3 0.0 collective-permute-done.2.got
  48.3 5.8 %all-to-all-done.4.grads = bf16[8,4,16,128]{3,2,1,0:T(8,128)(2,1)S(1)} async-done(((bf16[8,4,16,128]{3,2,1,0:T(8,128)(2,1)}), bf16[8,4,16,128]{3,2,1,0:T(8,128)(2,1)S(1)}, u32[]{:S(2)}, u32[]{:S(2)}) %all-to-all-start.4) | async-done | bytes 131104 | tf_op jit(solution)/shard_map/all_to_all | solution.py:196
  54.1 1.0 weight_term.1
  55.1 3.9 %all-to-all-start.5 = ((bf16[32,16,128]{2,1,0:T(8,128)(2,1)}), bf16[32,16,128]{2,1,0:T(8,128)(2,1)S(1)}, u32[]{:S(2)}, u32[]{:S(2)}) async-start(bf16[32,16,128]{2,1,0:T(8,128)(2,1)} %weight_term.1), calls=%async_computation.5 | async-start | bytes 262144 | tf_op jit(solution)/shard_map/all_to_all | solution.py:196
  59.0 3.1 %backward.1 = (f32[2,128,1024]{2,1,0:T(8,128)S(1)}, bf16[2,32,1024]{2,1,0:T(8,128)(2,1)S(1)}, bf16[2,32,1024]{2,1,0:T(8,128)(2,1)S(1)}) custom-call(bf16[8,4,16,128]{3,2,1,0:T(8,128)(2,1)S(1)} %all-to-all-done.4.grads, f32[2,256,128]{2,1,0:T(8,128)S(1)} %get-tuple-element.18.attn, bf16[2,128,1024]{2,1,0:T(8,128)(2,1)S(1)} %copy-done.1, ...), custom_call_target="tpu_custom_call" | custom-call | tf_op jit(solution)/shard_map/backward/pallas_call | solution.py:180
  62.1 6.2 %all-to-all-done.5.terms = bf16[32,16,128]{2,1,0:T(8,128)(2,1)S(1)} async-done(((bf16[32,16,128]{2,1,0:T(8,128)(2,1)}), bf16[32,16,128]{2,1,0:T(8,128)(2,1)S(1)}, u32[]{:S(2)}, u32[]{:S(2)}) %all-to-all-start.5) | async-done | bytes 131104 | tf_op jit(solution)/shard_map/all_to_all | solution.py:196
  68.3 0.7 add_plane.1
  69.0 13.2 %all-to-all-start.6 = ((bf16[12,16,128]{2,1,0:T(8,128)(2,1)}), bf16[12,16,128]{2,1,0:T(8,128)(2,1)S(1)}, u32[]{:S(2)}, u32[]{:S(2)}) async-start(bf16[12,16,128]{2,1,0:T(8,128)(2,1)} %add_plane.1), calls=%async_computation.6 | async-start | bytes 98304 | tf_op jit(solution)/shard_map/all_to_all | solution.py:196
  82.2 3.0 %collective-permute-start.3 = (bf16[2,32,1024]{2,1,0:T(8,128)(2,1)S(1)}, bf16[2,32,1024]{2,1,0:T(8,128)(2,1)S(1)}, u32[]{:S(2)}, u32[]{:S(2)}) collective-permute-start(bf16[2,32,1024]{2,1,0:T(8,128)(2,1)S(1)} %get-tuple-element.24), channel_id=1, source_target_pairs={{0,1},{1,2},{2,3},{3,4},{4,5},{5,6},{6,7},{7,8},{8,9},{9,10},{10,1... | collective-permute-start | bytes 393224 | tf_op jit(solution)/shard_map/ppermute | solution.py:286
  85.3 10.4 %collective-permute-start.4 = (bf16[2,32,1024]{2,1,0:T(8,128)(2,1)S(1)}, bf16[2,32,1024]{2,1,0:T(8,128)(2,1)S(1)}, u32[]{:S(2)}, u32[]{:S(2)}) collective-permute-start(bf16[2,32,1024]{2,1,0:T(8,128)(2,1)S(1)} %get-tuple-element.25), channel_id=1, source_target_pairs={{0,95},{1,0},{2,1},{3,2},{4,3},{5,4},{6,5},{7,6},{8,7},{9,8},{10,9... | collective-permute-start | bytes 393224 | tf_op jit(solution)/shard_map/ppermute | solution.py:285
  95.7 0.0 all-to-all-done.6.terms
  95.7 12.3 %conditional.1 = (bf16[32,16,128]{2,1,0:T(8,128)(2,1)S(1)}) conditional(s32[]{:T(128)} %bitcast.5, bf16[32,16,128]{2,1,0:T(8,128)(2,1)S(1)} %add_z.1, bf16[32,16,128]{2,1,0:T(8,128)(2,1)S(1)} %add_z.1), branch_computations={%region_0.1_spmd, %region_1.2_spmd} | conditional | bytes 1048584 | solution.py:288
  95.7 12.3 %all_to_all.34 = bf16[32,16,128]{2,1,0:T(8,128)(2,1)S(1)} all-to-all(bf16[32,16,128]{2,1,0:T(8,128)(2,1)S(1)} %param.1), channel_id=1, replica_groups=mesh['ylo'=4,'core'=2,'z'=12,'x'=4,'yhi'=2] {'x','ylo','yhi'}, dimensions={0} | all-to-all | bytes 262144 | tf_op jit(solution)/shard_map/cond/branch_1_fun/all_to_all | solution.py:196
  108.0 6.5 %collective-permute-start.5 = (bf16[32,16,128]{2,1,0:T(8,128)(2,1)S(1)}, bf16[32,16,128]{2,1,0:T(8,128)(2,1)S(1)}, u32[]{:S(2)}, u32[]{:S(2)}) collective-permute-start(bf16[32,16,128]{2,1,0:T(8,128)(2,1)S(1)} %get-tuple-element.29.mine), channel_id=1, source_target_pairs={{0,96},{96,0},{1,97},{97,1},{2,98},{98,2},{3,99},{99,3},{4,100},{1... | collective-permute-start | bytes 393224 | tf_op jit(solution)/shard_map/ppermute | solution.py:289
  114.5 0.0 collective-permute-done.3.from_prev
  114.5 0.0 collective-permute-done.4.from_next
  114.5 0.9 finish.1
  115.4 0.1 collective-permute-done.5.other
  115.5 0.8 assemble.1
  (4 shorter events, 0.1 us)
Async XLA Ops:
  0.6 38.7 %copy-start = (f32[128,100]{0,1:T(8,128)S(1)}, f32[128,100]{0,1:T(8,128)}, u32[]{:S(2)}) copy-start(f32[128,100]{0,1:T(8,128)} %param.12) | copy-start | bytes 153604
  0.6 28.5 %copy-start.1 = (bf16[2,128,1024]{2,1,0:T(8,128)(2,1)S(1)}, bf16[2,128,1024]{2,1,0:T(8,128)(2,1)}, u32[]{:S(2)}) copy-start(bf16[2,128,1024]{2,1,0:T(8,128)(2,1)} %own.3) | copy-start | bytes 1572868
  0.7 28.5 %copy-start.2 = (bf16[2,128,1024]{2,1,0:T(8,128)(2,1)S(1)}, bf16[2,128,1024]{2,1,0:T(8,128)(2,1)}, u32[]{:S(2)}) copy-start(bf16[2,128,1024]{2,1,0:T(8,128)(2,1)} %queries.3) | copy-start | bytes 1572868
  1.7 27.4 %collective-permute-start = (bf16[2,32,1024]{2,1,0:T(8,128)(2,1)S(1)}, bf16[2,32,1024]{2,1,0:T(8,128)(2,1)S(1)}, u32[]{:S(2)}, u32[]{:S(2)}) collective-permute-start(bf16[2,32,1024]{2,1,0:T(8,128)(2,1)S(1)} %get-tuple-element.28), channel_id=1, source_target_pairs={{0,1},{1,2},{2,3},{3,4},{4,5},{5,6},{6,7},{7,8},{8,9},{9,10},{10,1... | collective-permute-start | bytes 393224 | tf_op jit(solution)/shard_map/ppermute | solution.py:221
  10.0 19.1 %collective-permute-start.1 = (bf16[2,32,1024]{2,1,0:T(8,128)(2,1)S(1)}, bf16[2,32,1024]{2,1,0:T(8,128)(2,1)S(1)}, u32[]{:S(2)}, u32[]{:S(2)}) collective-permute-start(bf16[2,32,1024]{2,1,0:T(8,128)(2,1)S(1)} %get-tuple-element.27), channel_id=1, source_target_pairs={{0,95},{1,0},{2,1},{3,2},{4,3},{5,4},{6,5},{7,6},{8,7},{9,8},{10,9... | collective-permute-start | bytes 393224 | tf_op jit(solution)/shard_map/ppermute | solution.py:222
  27.0 1.0 copy-start.3
  31.7 5.6 %copy-start.4 = (f32[100]{0:T(128)S(1)}, f32[100]{0:T(128)}, u32[]{:S(2)}) copy-start(f32[100]{0:T(128)} %param.14) | copy-start | bytes 1204
  31.7 11.4 %all-to-all-start.3 = ((f32[8,2,16,128]{3,2,1,0:T(8,128)}), f32[8,2,16,128]{3,2,1,0:T(8,128)S(1)}, u32[]{:S(2)}, u32[]{:S(2)}) async-start(f32[8,2,16,128]{3,2,1,0:T(8,128)} %get-tuple-element.17), calls=%async_computation.3 | async-start | bytes 262144 | tf_op jit(solution)/shard_map/all_to_all | solution.py:196
  37.3 11.0 %collective-permute-start.2 = (bf16[2,128,512]{2,1,0:T(8,128)(2,1)S(1)}, bf16[2,128,512]{2,1,0:T(8,128)(2,1)S(1)}, u32[]{:S(2)}, u32[]{:S(2)}) collective-permute-start(bf16[2,128,512]{2,1,0:T(8,128)(2,1)S(1)} %get-tuple-element.21), channel_id=1, source_target_pairs={{0,96},{96,0},{1,97},{97,1},{2,98},{98,2},{3,99},{99,3},{4,100},{1... | collective-permute-start | bytes 786440 | tf_op jit(solution)/shard_map/ppermute | solution.py:254
  44.0 10.1 %all-to-all-start.4 = ((bf16[8,4,16,128]{3,2,1,0:T(8,128)(2,1)}), bf16[8,4,16,128]{3,2,1,0:T(8,128)(2,1)S(1)}, u32[]{:S(2)}, u32[]{:S(2)}) async-start(bf16[8,4,16,128]{3,2,1,0:T(8,128)(2,1)} %crps.1), calls=%async_computation.4 | async-start | bytes 262144 | tf_op jit(solution)/shard_map/all_to_all | solution.py:196
  55.1 13.2 %all-to-all-start.5 = ((bf16[32,16,128]{2,1,0:T(8,128)(2,1)}), bf16[32,16,128]{2,1,0:T(8,128)(2,1)S(1)}, u32[]{:S(2)}, u32[]{:S(2)}) async-start(bf16[32,16,128]{2,1,0:T(8,128)(2,1)} %weight_term.1), calls=%async_computation.5 | async-start | bytes 262144 | tf_op jit(solution)/shard_map/all_to_all | solution.py:196
  69.0 26.7 %all-to-all-start.6 = ((bf16[12,16,128]{2,1,0:T(8,128)(2,1)}), bf16[12,16,128]{2,1,0:T(8,128)(2,1)S(1)}, u32[]{:S(2)}, u32[]{:S(2)}) async-start(bf16[12,16,128]{2,1,0:T(8,128)(2,1)} %add_plane.1), calls=%async_computation.6 | async-start | bytes 98304 | tf_op jit(solution)/shard_map/all_to_all | solution.py:196
  82.2 32.3 %collective-permute-start.3 = (bf16[2,32,1024]{2,1,0:T(8,128)(2,1)S(1)}, bf16[2,32,1024]{2,1,0:T(8,128)(2,1)S(1)}, u32[]{:S(2)}, u32[]{:S(2)}) collective-permute-start(bf16[2,32,1024]{2,1,0:T(8,128)(2,1)S(1)} %get-tuple-element.24), channel_id=1, source_target_pairs={{0,1},{1,2},{2,3},{3,4},{4,5},{5,6},{6,7},{7,8},{8,9},{9,10},{10,1... | collective-permute-start | bytes 393224 | tf_op jit(solution)/shard_map/ppermute | solution.py:286
  85.3 29.2 %collective-permute-start.4 = (bf16[2,32,1024]{2,1,0:T(8,128)(2,1)S(1)}, bf16[2,32,1024]{2,1,0:T(8,128)(2,1)S(1)}, u32[]{:S(2)}, u32[]{:S(2)}) collective-permute-start(bf16[2,32,1024]{2,1,0:T(8,128)(2,1)S(1)} %get-tuple-element.25), channel_id=1, source_target_pairs={{0,95},{1,0},{2,1},{3,2},{4,3},{5,4},{6,5},{7,6},{8,7},{9,8},{10,9... | collective-permute-start | bytes 393224 | tf_op jit(solution)/shard_map/ppermute | solution.py:285
  108.0 7.4 %collective-permute-start.5 = (bf16[32,16,128]{2,1,0:T(8,128)(2,1)S(1)}, bf16[32,16,128]{2,1,0:T(8,128)(2,1)S(1)}, u32[]{:S(2)}, u32[]{:S(2)}) collective-permute-start(bf16[32,16,128]{2,1,0:T(8,128)(2,1)S(1)} %get-tuple-element.29.mine), channel_id=1, source_target_pairs={{0,96},{96,0},{1,97},{97,1},{2,98},{98,2},{3,99},{99,3},{4,100},{1... | collective-permute-start | bytes 393224 | tf_op jit(solution)/shard_map/ppermute | solution.py:289

commit v4 on v3

--- a/solution.py
+++ b/solution.py
@@ -39,24 +39,31 @@
     window[nodes + reach : nodes + 2 * reach] = high[m]
 
 
+def prepare_kernel(slots, own, queries, count_out, scores_out):
+    rows, points = count_out.shape
+    place = lax.broadcasted_iota(jnp.int32, (rows, points), 0)
+    count = jnp.zeros((rows, points), f32)
+    for slot in range(slots.shape[0]):
+        count = count + (place == slots[slot : slot + 1]).astype(f32)
+    count_out[...] = count
+    for m in range(queries.shape[0]):
+        scores_out[m] = dot(own[m], queries[m], 1, 1)
+
+
 def forward_kernel(
-    scale, core, slots, own, low, high, queries, weight, attn_out, keep_out, give_out, pred_out, window
+    scale, core, counts, near, own, low, high, queries, weight,
+    attn_out, keep_out, give_out, pred_out, window,
 ):
     members, points, width = queries.shape
     half = width // 2
     here = core[0] == 0
-    rows = window.shape[0]
-    nodes, reach = own.shape[1], low.shape[1]
+    nodes = own.shape[1]
     share = pred_out.shape[2]
-    window[nodes + 2 * reach :] = jnp.zeros((rows - nodes - 2 * reach, window.shape[1]), bf16)
-    place = lax.broadcasted_iota(jnp.int32, (rows, points), 0)
-    count = jnp.zeros((rows, points), f32)
-    for slot in range(slots.shape[0]):
-        count = count + (place == slots[slot : slot + 1]).astype(f32)
+    count = counts[...]
     used = count > 0.0
     for m in range(members):
         fill_window(window, m, own, low, high)
-        scores = dot(window[...], queries[m], 1, 1) * scale
+        scores = jnp.concatenate([near[m], dot(window[nodes:], queries[m], 1, 1)]) * scale
         scores = jnp.where(used, scores, -1e30)
         top = jnp.max(scores, axis=0, keepdims=True)
         raised = count * jnp.exp(scores - top)
@@ -143,9 +150,7 @@
     owners, _, share, lanes = grads.shape
     members = queries.shape[0]
     points = owners * share
-    rows = window.shape[0]
     nodes, reach = own.shape[1], low.shape[1]
-    window[nodes + 2 * reach :] = jnp.zeros((rows - nodes - 2 * reach, window.shape[1]), bf16)
     for m in range(members):
         fill_window(window, m, own, low, high)
         g = grads[:, m].reshape(points, lanes)
@@ -233,10 +238,19 @@
     area = lax.dynamic_slice_in_dim(area_weight, start, share, 0)
     weighting = jnp.pad(area[:, None] * var_weight[None, :], pad_lanes)
 
-    window_rows = 2 * LANES
+    window_rows = nodes + 2 * reach
     window = pltpu.VMEM((window_rows, width), bf16)
     core = lax.axis_index("core").astype(jnp.int32).reshape(1)
     swap = [(0, 1), (1, 0)]
+    counts, near = call(
+        prepare_kernel,
+        [
+            jax.ShapeDtypeStruct((window_rows, points), f32),
+            jax.ShapeDtypeStruct((members, nodes, points), f32),
+        ],
+        (slots, latents, queries),
+        name="prepare",
+    )
     attn, keep, give, pred = call(
         functools.partial(forward_kernel, scale),
         [
@@ -245,7 +259,7 @@
             jax.ShapeDtypeStruct((members, points, width // 2), bf16),
             jax.ShapeDtypeStruct((owners, members, share, LANES), f32),
         ],
-        (core, slots, latents, low, high, queries, weight),
+        (core, counts, near, latents, low, high, queries, weight),
         [window],
         name="forward",
         scalars=1,

time: 117 us -> 117 us (level)
  local copies, waits for them, and re-layouts: 2.97 us -> 4.26 us
    unnamed x11 -> x17, local copies, waits for them, and re-layouts: 0.09 us -> 3.01 us
    pallas_call x8 -> x9, Pallas kernels: 9.84 us -> 9.24 us  [call(): pl.pallas_call(kernel, out_shape=out_shape, in_specs=[smem] * scalars + [...]
  transfers between devices with their start and end apart: 10 -> 10, of which waited for: 5 -> 4; matrix products, arithmetic and copies ran while one was open for 2% -> 0% of each run, Pallas kernels for 4% -> 4%
where the time goes in v4:
time: 117 us; the launch traced here: 116 us
  starting transfers between devices  72.7 us (62%)
  waiting for transfers between devices  16.4 us (14%)
  blocking collectives  12.3 us (11%)
  Pallas kernels  9.24 us (8%)
  local copies, waits for them, and re-layouts  4.26 us (4%)
    all_to_all x4, starting transfers between devices, exchange(): return lax.all_to_all(x, axes, 0, 0, tiled=True)  26.3 us
    all_to_all x4, waiting for transfers between devices, exchange(): return lax.all_to_all(x, axes, 0, 0, tiled=True)  16.3 us
    ppermute x1, starting transfers between devices, local(): high = lax.ppermute(latents[:, :reach], SHARD, backward)  16.2 us
    all_to_all x1, blocking collectives, exchange(): return lax.all_to_all(x, axes, 0, 0, tiled=True)  12.3 us
    ppermute x1, starting transfers between devices, local(): from_next = lax.ppermute(low_part, SHARD, backward)  10.4 us
    pallas_call x9, Pallas kernels, call(): pl.pallas_call(kernel, out_shape=out_shape, in_specs=[smem] * scalars + [...  9.24 us
    ppermute x1, starting transfers between devices, local(): low = lax.ppermute(latents[:, nodes - reach:], SHARD, forward)  8.28 us
    ppermute x1, starting transfers between devices, local(): other = lax.ppermute(mine, 'core', swap)  6.46 us
  transfers between devices with their start and end apart: 10, of which 4 were waited for; matrix products, arithmetic and copies ran while one was open for 0% of the time, Pallas kernels for 4%

profile of v4, /device:TPU:1, one launch (start us, length us, event | category | flops | bytes accessed | tf_op | source)
XLA Modules:
  0.0 115.9 jit_solution(14443513540997228658)
XLA Ops:
  0.6 0.0 copy-start
  0.6 0.0 copy-start.1
  0.7 1.1 fusion.2
  1.7 8.3 %collective-permute-start = (bf16[2,32,1024]{2,1,0:T(8,128)(2,1)S(1)}, bf16[2,32,1024]{2,1,0:T(8,128)(2,1)S(1)}, u32[]{:S(2)}, u32[]{:S(2)}) collective-permute-start(bf16[2,32,1024]{2,1,0:T(8,128)(2,1)S(1)} %get-tuple-element.32), channel_id=1, source_target_pairs={{0,1},{1,2},{2,3},{3,4},{4,5},{5,6},{6,7},{7,8},{8,9},{9,10},{10,1... | collective-permute-start | bytes 393224 | tf_op jit(solution)/shard_map/ppermute | solution.py:226
  10.0 16.2 %collective-permute-start.1 = (bf16[2,32,1024]{2,1,0:T(8,128)(2,1)S(1)}, bf16[2,32,1024]{2,1,0:T(8,128)(2,1)S(1)}, u32[]{:S(2)}, u32[]{:S(2)}) collective-permute-start(bf16[2,32,1024]{2,1,0:T(8,128)(2,1)S(1)} %get-tuple-element.31), channel_id=1, source_target_pairs={{0,95},{1,0},{2,1},{3,2},{4,3},{5,4},{6,5},{7,6},{8,7},{9,8},{10,9... | collective-permute-start | bytes 393224 | tf_op jit(solution)/shard_map/ppermute | solution.py:227
  26.3 0.0 copy-start.5
  26.3 0.7 copy-done.5
  27.0 0.0 copy-done.1
  27.0 0.0 copy-start.2
  27.0 1.0 copy-done.2
  28.0 0.4 prepare.1
  28.4 0.6 copy-done.4
  29.0 0.0 copy-start.7
  29.0 0.6 copy-done.7
  29.6 0.1 dynamic_slice.7
  29.7 0.0 collective-permute-done.low
  29.7 0.0 collective-permute-done.1.high
  29.7 0.0 copy-done.3
  29.7 2.2 %forward.1 = (f32[2,192,128]{2,1,0:T(8,128)S(1)}, bf16[2,128,512]{2,1,0:T(8,128)(2,1)S(1)}, bf16[2,128,512]{2,1,0:T(8,128)(2,1)S(1)}, f32[8,2,16,128]{3,2,1,0:T(8,128)}) custom-call(s32[1]{0:T(128)} %bitcast.2.core, f32[192,128]{1,0:T(8,128)S(1)} %get-tuple-element.19.counts, f32[2,128,128]{2,1,0:T(8,128)S(1)} %get-tuple-element.20.near, ...), custom_call_target="tpu_custom_call" | custom-call | tf_op jit(solution)/shard_map/forward/pallas_call | solution.py:185
  31.9 5.0 %all-to-all-start.3 = ((f32[8,2,16,128]{3,2,1,0:T(8,128)}), f32[8,2,16,128]{3,2,1,0:T(8,128)S(1)}, u32[]{:S(2)}, u32[]{:S(2)}) async-start(f32[8,2,16,128]{3,2,1,0:T(8,128)} %get-tuple-element.21), calls=%async_computation.3 | async-start | bytes 262144 | tf_op jit(solution)/shard_map/all_to_all | solution.py:201
  36.9 0.0 copy-done.6
  36.9 0.1 broadcast_multiply_fusion
  37.0 2.0 %collective-permute-start.2 = (bf16[2,128,512]{2,1,0:T(8,128)(2,1)S(1)}, bf16[2,128,512]{2,1,0:T(8,128)(2,1)S(1)}, u32[]{:S(2)}, u32[]{:S(2)}) collective-permute-start(bf16[2,128,512]{2,1,0:T(8,128)(2,1)S(1)} %get-tuple-element.25), channel_id=1, source_target_pairs={{0,96},{96,0},{1,97},{97,1},{2,98},{98,2},{3,99},{99,3},{4,100},{1... | collective-permute-start | bytes 786440 | tf_op jit(solution)/shard_map/ppermute | solution.py:268
  39.0 0.0 copy-done
  39.0 0.1 constant_dynamic-slice_fusion
  39.1 0.1 copy.14
  39.2 3.6 %all-to-all-done.3.rows = f32[8,2,16,128]{3,2,1,0:T(8,128)S(1)} async-done(((f32[8,2,16,128]{3,2,1,0:T(8,128)}), f32[8,2,16,128]{3,2,1,0:T(8,128)S(1)}, u32[]{:S(2)}, u32[]{:S(2)}) %all-to-all-start.3) | async-done | bytes 131104 | tf_op jit(solution)/shard_map/all_to_all | solution.py:201
  42.7 0.9 crps.1
  43.7 4.2 %all-to-all-start.4 = ((bf16[8,4,16,128]{3,2,1,0:T(8,128)(2,1)}), bf16[8,4,16,128]{3,2,1,0:T(8,128)(2,1)S(1)}, u32[]{:S(2)}, u32[]{:S(2)}) async-start(bf16[8,4,16,128]{3,2,1,0:T(8,128)(2,1)} %crps.1), calls=%async_computation.4 | async-start | bytes 262144 | tf_op jit(solution)/shard_map/all_to_all | solution.py:201
  47.9 0.0 collective-permute-done.2.got
  47.9 5.8 %all-to-all-done.4.grads = bf16[8,4,16,128]{3,2,1,0:T(8,128)(2,1)S(1)} async-done(((bf16[8,4,16,128]{3,2,1,0:T(8,128)(2,1)}), bf16[8,4,16,128]{3,2,1,0:T(8,128)(2,1)S(1)}, u32[]{:S(2)}, u32[]{:S(2)}) %all-to-all-start.4) | async-done | bytes 131104 | tf_op jit(solution)/shard_map/all_to_all | solution.py:201
  53.8 1.0 weight_term.1
  54.7 3.9 %all-to-all-start.5 = ((bf16[32,16,128]{2,1,0:T(8,128)(2,1)}), bf16[32,16,128]{2,1,0:T(8,128)(2,1)S(1)}, u32[]{:S(2)}, u32[]{:S(2)}) async-start(bf16[32,16,128]{2,1,0:T(8,128)(2,1)} %weight_term.1), calls=%async_computation.5 | async-start | bytes 262144 | tf_op jit(solution)/shard_map/all_to_all | solution.py:201
  58.6 2.4 %backward.1 = (f32[2,128,1024]{2,1,0:T(8,128)S(1)}, bf16[2,32,1024]{2,1,0:T(8,128)(2,1)S(1)}, bf16[2,32,1024]{2,1,0:T(8,128)(2,1)S(1)}) custom-call(bf16[8,4,16,128]{3,2,1,0:T(8,128)(2,1)S(1)} %all-to-all-done.4.grads, f32[2,192,128]{2,1,0:T(8,128)S(1)} %get-tuple-element.22.attn, bf16[2,128,1024]{2,1,0:T(8,128)(2,1)S(1)} %copy-done.1, ...), custom_call_target="tpu_custom_call" | custom-call | tf_op jit(solution)/shard_map/backward/pallas_call | solution.py:185
  61.1 6.9 %all-to-all-done.5.terms = bf16[32,16,128]{2,1,0:T(8,128)(2,1)S(1)} async-done(((bf16[32,16,128]{2,1,0:T(8,128)(2,1)}), bf16[32,16,128]{2,1,0:T(8,128)(2,1)S(1)}, u32[]{:S(2)}, u32[]{:S(2)}) %all-to-all-start.5) | async-done | bytes 131104 | tf_op jit(solution)/shard_map/all_to_all | solution.py:201
  68.0 0.7 add_plane.1
  68.6 13.2 %all-to-all-start.6 = ((bf16[12,16,128]{2,1,0:T(8,128)(2,1)}), bf16[12,16,128]{2,1,0:T(8,128)(2,1)S(1)}, u32[]{:S(2)}, u32[]{:S(2)}) async-start(bf16[12,16,128]{2,1,0:T(8,128)(2,1)} %add_plane.1), calls=%async_computation.6 | async-start | bytes 98304 | tf_op jit(solution)/shard_map/all_to_all | solution.py:201
  81.9 3.0 %collective-permute-start.3 = (bf16[2,32,1024]{2,1,0:T(8,128)(2,1)S(1)}, bf16[2,32,1024]{2,1,0:T(8,128)(2,1)S(1)}, u32[]{:S(2)}, u32[]{:S(2)}) collective-permute-start(bf16[2,32,1024]{2,1,0:T(8,128)(2,1)S(1)} %get-tuple-element.28), channel_id=1, source_target_pairs={{0,1},{1,2},{2,3},{3,4},{4,5},{5,6},{6,7},{7,8},{8,9},{9,10},{10,1... | collective-permute-start | bytes 393224 | tf_op jit(solution)/shard_map/ppermute | solution.py:300
  84.9 10.4 %collective-permute-start.4 = (bf16[2,32,1024]{2,1,0:T(8,128)(2,1)S(1)}, bf16[2,32,1024]{2,1,0:T(8,128)(2,1)S(1)}, u32[]{:S(2)}, u32[]{:S(2)}) collective-permute-start(bf16[2,32,1024]{2,1,0:T(8,128)(2,1)S(1)} %get-tuple-element.29), channel_id=1, source_target_pairs={{0,95},{1,0},{2,1},{3,2},{4,3},{5,4},{6,5},{7,6},{8,7},{9,8},{10,9... | collective-permute-start | bytes 393224 | tf_op jit(solution)/shard_map/ppermute | solution.py:299
  95.3 0.0 all-to-all-done.6.terms
  95.3 12.3 %conditional.1 = (bf16[32,16,128]{2,1,0:T(8,128)(2,1)S(1)}) conditional(s32[]{:T(128)} %bitcast.5, bf16[32,16,128]{2,1,0:T(8,128)(2,1)S(1)} %add_z.1, bf16[32,16,128]{2,1,0:T(8,128)(2,1)S(1)} %add_z.1), branch_computations={%region_0.1_spmd, %region_1.2_spmd} | conditional | bytes 1048584 | solution.py:302
  95.4 12.3 %all_to_all.34 = bf16[32,16,128]{2,1,0:T(8,128)(2,1)S(1)} all-to-all(bf16[32,16,128]{2,1,0:T(8,128)(2,1)S(1)} %param.1), channel_id=1, replica_groups=mesh['ylo'=4,'core'=2,'z'=12,'x'=4,'yhi'=2] {'x','ylo','yhi'}, dimensions={0} | all-to-all | bytes 262144 | tf_op jit(solution)/shard_map/cond/branch_1_fun/all_to_all | solution.py:201
  107.7 6.5 %collective-permute-start.5 = (bf16[32,16,128]{2,1,0:T(8,128)(2,1)S(1)}, bf16[32,16,128]{2,1,0:T(8,128)(2,1)S(1)}, u32[]{:S(2)}, u32[]{:S(2)}) collective-permute-start(bf16[32,16,128]{2,1,0:T(8,128)(2,1)S(1)} %get-tuple-element.33.mine), channel_id=1, source_target_pairs={{0,96},{96,0},{1,97},{97,1},{2,98},{98,2},{3,99},{99,3},{4,100},{1... | collective-permute-start | bytes 393224 | tf_op jit(solution)/shard_map/ppermute | solution.py:303
  114.1 0.0 collective-permute-done.3.from_prev
  114.2 0.0 collective-permute-done.4.from_next
  114.2 0.9 finish.1
  115.0 0.1 collective-permute-done.5.other
  115.1 0.8 assemble.1
  (8 shorter events, 0.1 us)
Async XLA Ops:
  0.6 38.4 %copy-start = (f32[128,100]{0,1:T(8,128)S(1)}, f32[128,100]{0,1:T(8,128)}, u32[]{:S(2)}) copy-start(f32[128,100]{0,1:T(8,128)} %param.12) | copy-start | bytes 153604
  0.6 26.3 %copy-start.1 = (bf16[2,128,1024]{2,1,0:T(8,128)(2,1)S(1)}, bf16[2,128,1024]{2,1,0:T(8,128)(2,1)}, u32[]{:S(2)}) copy-start(bf16[2,128,1024]{2,1,0:T(8,128)(2,1)} %own.5) | copy-start | bytes 1572868
  1.7 28.0 %collective-permute-start = (bf16[2,32,1024]{2,1,0:T(8,128)(2,1)S(1)}, bf16[2,32,1024]{2,1,0:T(8,128)(2,1)S(1)}, u32[]{:S(2)}, u32[]{:S(2)}) collective-permute-start(bf16[2,32,1024]{2,1,0:T(8,128)(2,1)S(1)} %get-tuple-element.32), channel_id=1, source_target_pairs={{0,1},{1,2},{2,3},{3,4},{4,5},{5,6},{6,7},{7,8},{8,9},{9,10},{10,1... | collective-permute-start | bytes 393224 | tf_op jit(solution)/shard_map/ppermute | solution.py:226
  10.0 19.7 %collective-permute-start.1 = (bf16[2,32,1024]{2,1,0:T(8,128)(2,1)S(1)}, bf16[2,32,1024]{2,1,0:T(8,128)(2,1)S(1)}, u32[]{:S(2)}, u32[]{:S(2)}) collective-permute-start(bf16[2,32,1024]{2,1,0:T(8,128)(2,1)S(1)} %get-tuple-element.31), channel_id=1, source_target_pairs={{0,95},{1,0},{2,1},{3,2},{4,3},{5,4},{6,5},{7,6},{8,7},{9,8},{10,9... | collective-permute-start | bytes 393224 | tf_op jit(solution)/shard_map/ppermute | solution.py:227
  26.3 0.7 copy-start.5
  27.0 1.0 copy-start.2
  28.0 0.9 copy-start.4
  28.0 1.7 %copy-start.3 = (bf16[2,128,1024]{2,1,0:T(8,128)(2,1)S(1)}, bf16[2,128,1024]{2,1,0:T(8,128)(2,1)}, u32[]{:S(2)}) copy-start(bf16[2,128,1024]{2,1,0:T(8,128)(2,1)} %queries.5) | copy-start | bytes 1572868
  29.0 0.7 copy-start.7
  31.9 5.0 %copy-start.6 = (f32[100]{0:T(128)S(1)}, f32[100]{0:T(128)}, u32[]{:S(2)}) copy-start(f32[100]{0:T(128)} %param.14) | copy-start | bytes 1204
  31.9 10.8 %all-to-all-start.3 = ((f32[8,2,16,128]{3,2,1,0:T(8,128)}), f32[8,2,16,128]{3,2,1,0:T(8,128)S(1)}, u32[]{:S(2)}, u32[]{:S(2)}) async-start(f32[8,2,16,128]{3,2,1,0:T(8,128)} %get-tuple-element.21), calls=%async_computation.3 | async-start | bytes 262144 | tf_op jit(solution)/shard_map/all_to_all | solution.py:201
  37.0 11.0 %collective-permute-start.2 = (bf16[2,128,512]{2,1,0:T(8,128)(2,1)S(1)}, bf16[2,128,512]{2,1,0:T(8,128)(2,1)S(1)}, u32[]{:S(2)}, u32[]{:S(2)}) collective-permute-start(bf16[2,128,512]{2,1,0:T(8,128)(2,1)S(1)} %get-tuple-element.25), channel_id=1, source_target_pairs={{0,96},{96,0},{1,97},{97,1},{2,98},{98,2},{3,99},{99,3},{4,100},{1... | collective-permute-start | bytes 786440 | tf_op jit(solution)/shard_map/ppermute | solution.py:268
  43.7 10.1 %all-to-all-start.4 = ((bf16[8,4,16,128]{3,2,1,0:T(8,128)(2,1)}), bf16[8,4,16,128]{3,2,1,0:T(8,128)(2,1)S(1)}, u32[]{:S(2)}, u32[]{:S(2)}) async-start(bf16[8,4,16,128]{3,2,1,0:T(8,128)(2,1)} %crps.1), calls=%async_computation.4 | async-start | bytes 262144 | tf_op jit(solution)/shard_map/all_to_all | solution.py:201
  54.7 13.2 %all-to-all-start.5 = ((bf16[32,16,128]{2,1,0:T(8,128)(2,1)}), bf16[32,16,128]{2,1,0:T(8,128)(2,1)S(1)}, u32[]{:S(2)}, u32[]{:S(2)}) async-start(bf16[32,16,128]{2,1,0:T(8,128)(2,1)} %weight_term.1), calls=%async_computation.5 | async-start | bytes 262144 | tf_op jit(solution)/shard_map/all_to_all | solution.py:201
  68.6 26.7 %all-to-all-start.6 = ((bf16[12,16,128]{2,1,0:T(8,128)(2,1)}), bf16[12,16,128]{2,1,0:T(8,128)(2,1)S(1)}, u32[]{:S(2)}, u32[]{:S(2)}) async-start(bf16[12,16,128]{2,1,0:T(8,128)(2,1)} %add_plane.1), calls=%async_computation.6 | async-start | bytes 98304 | tf_op jit(solution)/shard_map/all_to_all | solution.py:201
  81.9 32.3 %collective-permute-start.3 = (bf16[2,32,1024]{2,1,0:T(8,128)(2,1)S(1)}, bf16[2,32,1024]{2,1,0:T(8,128)(2,1)S(1)}, u32[]{:S(2)}, u32[]{:S(2)}) collective-permute-start(bf16[2,32,1024]{2,1,0:T(8,128)(2,1)S(1)} %get-tuple-element.28), channel_id=1, source_target_pairs={{0,1},{1,2},{2,3},{3,4},{4,5},{5,6},{6,7},{7,8},{8,9},{9,10},{10,1... | collective-permute-start | bytes 393224 | tf_op jit(solution)/shard_map/ppermute | solution.py:300
  84.9 29.2 %collective-permute-start.4 = (bf16[2,32,1024]{2,1,0:T(8,128)(2,1)S(1)}, bf16[2,32,1024]{2,1,0:T(8,128)(2,1)S(1)}, u32[]{:S(2)}, u32[]{:S(2)}) collective-permute-start(bf16[2,32,1024]{2,1,0:T(8,128)(2,1)S(1)} %get-tuple-element.29), channel_id=1, source_target_pairs={{0,95},{1,0},{2,1},{3,2},{4,3},{5,4},{6,5},{7,6},{8,7},{9,8},{10,9... | collective-permute-start | bytes 393224 | tf_op jit(solution)/shard_map/ppermute | solution.py:299
  107.7 7.4 %collective-permute-start.5 = (bf16[32,16,128]{2,1,0:T(8,128)(2,1)S(1)}, bf16[32,16,128]{2,1,0:T(8,128)(2,1)S(1)}, u32[]{:S(2)}, u32[]{:S(2)}) collective-permute-start(bf16[32,16,128]{2,1,0:T(8,128)(2,1)S(1)} %get-tuple-element.33.mine), channel_id=1, source_target_pairs={{0,96},{96,0},{1,97},{97,1},{2,98},{98,2},{3,99},{99,3},{4,100},{1... | collective-permute-start | bytes 393224 | tf_op jit(solution)/shard_map/ppermute | solution.py:303

commit v5 on v4

--- a/solution.py
+++ b/solution.py
@@ -145,8 +145,9 @@
 
 
 def backward_kernel(
-    scale, grads, attn, own, low, high, queries, weight, own_out, low_out, high_out, window
+    scale, side, grads, attn, own, low, high, queries, weight, own_out, even_out, odd_out, window
 ):
+    first = side[0] == 0
     owners, _, share, lanes = grads.shape
     members = queries.shape[0]
     points = owners * share
@@ -167,16 +168,20 @@
             + dot(s_low, queries[m], 1, 0)
         )
         own_out[m] = total[:nodes]
-        low_out[m] = total[nodes : nodes + reach].astype(bf16)
-        high_out[m] = total[nodes + reach : nodes + 2 * reach].astype(bf16)
-
-
-def finish_kernel(own, from_prev, from_next, out):
-    nodes, reach = own.shape[1], from_prev.shape[1]
+        lower = total[nodes : nodes + reach].astype(bf16)
+        upper = total[nodes + reach : nodes + 2 * reach].astype(bf16)
+        even_out[m] = jnp.where(first, upper, lower)
+        odd_out[m] = jnp.where(first, lower, upper)
+
+
+def finish_kernel(side, own, even, odd, out):
+    nodes, reach = own.shape[1], even.shape[1]
+    first = side[0] == 0
     for m in range(own.shape[0]):
-        out[m, :reach] = (own[m, :reach] + from_prev[m].astype(f32)).astype(bf16)
+        e, o = even[m].astype(f32), odd[m].astype(f32)
+        out[m, :reach] = (own[m, :reach] + jnp.where(first, o, e)).astype(bf16)
         out[m, reach : nodes - reach] = own[m, reach : nodes - reach].astype(bf16)
-        out[m, nodes - reach :] = (own[m, nodes - reach :] + from_next[m].astype(f32)).astype(bf16)
+        out[m, nodes - reach :] = (own[m, nodes - reach :] + jnp.where(first, e, o)).astype(bf16)
 
 
 def call(kernel, out_shape, args, scratch=(), name=None, scalars=0):
@@ -284,20 +289,24 @@
     )
     term = exchange(term, SPREAD)
 
-    own_part, low_part, high_part = call(
+    side = lax.axis_index("yhi").astype(jnp.int32).reshape(1)
+    own_part, even_part, odd_part = call(
         functools.partial(backward_kernel, scale),
         [
             jax.ShapeDtypeStruct((members, nodes, width), f32),
             jax.ShapeDtypeStruct((members, reach, width), bf16),
             jax.ShapeDtypeStruct((members, reach, width), bf16),
         ],
-        (grads, attn, latents, low, high, queries, weight),
+        (side, grads, attn, latents, low, high, queries, weight),
         [window],
         name="backward",
-    )
-    term, low_part, high_part = lax.optimization_barrier((term, low_part, high_part))
-    from_next = lax.ppermute(low_part, SHARD, backward)
-    from_prev = lax.ppermute(high_part, SHARD, forward)
+        scalars=1,
+    )
+    term, even_part, odd_part = lax.optimization_barrier((term, even_part, odd_part))
+    even_pairs = [(i, i ^ 1) for i in range(shards)]
+    odd_pairs = [(i, (i + (1 if i % 2 else -1)) % shards) for i in range(shards)]
+    odd_back = lax.ppermute(odd_part, SHARD, odd_pairs)
+    even_back = lax.ppermute(even_part, SHARD, even_pairs)
     piece = exchange(add_up(term, lax.axis_size("z"), "add_plane"), "z")
     mine = lax.cond(var_weight[0] > 0.0, whole_exchange, split_exchange, add_up(piece, pieces, "add_z"))
     other = lax.ppermute(mine, "core", swap)
@@ -312,8 +321,9 @@
     latent_grad = call(
         finish_kernel,
         jax.ShapeDtypeStruct(latents.shape, bf16),
-        (own_part, from_prev, from_next),
+        (side, own_part, even_back, odd_back),
         name="finish",
+        scalars=1,
     )
     return latent_grad, proj_grad
 

time: 117 us -> 116 us (level)
    ppermute x2, starting transfers between devices: 13.4 us -> 12.2 us  [the longest x1 9.16 us: local(): odd_back = lax.ppermute(odd_part, SHARD, odd_pairs)]
  transfers between devices with their start and end apart: 10 -> 10, of which waited for: 4 -> 3; matrix products, arithmetic and copies ran while one was open for 0% -> 0% of each run, Pallas kernels for 4% -> 4%
where the time goes in v5:
time: 116 us; the launch traced here: 115 us
  starting transfers between devices  71.7 us (62%)
  waiting for transfers between devices  16.4 us (14%)
  blocking collectives  12.3 us (11%)
  Pallas kernels  9.26 us (8%)
  local copies, waits for them, and re-layouts  4.28 us (4%)
    all_to_all x4, starting transfers between devices, exchange(): return lax.all_to_all(x, axes, 0, 0, tiled=True)  26.3 us
    all_to_all x4, waiting for transfers between devices, exchange(): return lax.all_to_all(x, axes, 0, 0, tiled=True)  16.3 us
    ppermute x1, starting transfers between devices, local(): high = lax.ppermute(latents[:, :reach], SHARD, backward)  16.2 us
    all_to_all x1, blocking collectives, exchange(): return lax.all_to_all(x, axes, 0, 0, tiled=True)  12.3 us
    pallas_call x9, Pallas kernels, call(): pl.pallas_call(kernel, out_shape=out_shape, in_specs=[smem] * scalars + [...  9.26 us
    ppermute x1, starting transfers between devices, local(): odd_back = lax.ppermute(odd_part, SHARD, odd_pairs)  9.16 us
    ppermute x1, starting transfers between devices, local(): low = lax.ppermute(latents[:, nodes - reach:], SHARD, forward)  8.28 us
    ppermute x1, starting transfers between devices, local(): other = lax.ppermute(mine, 'core', swap)  6.73 us
  transfers between devices with their start and end apart: 10, of which 3 were waited for; matrix products, arithmetic and copies ran while one was open for 0% of the time, Pallas kernels for 4%

profile of v5, /device:TPU:1, one launch (start us, length us, event | category | flops | bytes accessed | tf_op | source)
XLA Modules:
  0.0 114.9 jit_solution(16732020083492168207)
XLA Ops:
  0.6 0.0 copy-start
  0.6 0.0 copy-start.1
  0.7 1.1 fusion.2
  1.7 8.3 %collective-permute-start = (bf16[2,32,1024]{2,1,0:T(8,128)(2,1)S(1)}, bf16[2,32,1024]{2,1,0:T(8,128)(2,1)S(1)}, u32[]{:S(2)}, u32[]{:S(2)}) collective-permute-start(bf16[2,32,1024]{2,1,0:T(8,128)(2,1)S(1)} %get-tuple-element.32), channel_id=1, source_target_pairs={{0,1},{1,2},{2,3},{3,4},{4,5},{5,6},{6,7},{7,8},{8,9},{9,10},{10,1... | collective-permute-start | bytes 393224 | tf_op jit(solution)/shard_map/ppermute | solution.py:231
  10.0 16.2 %collective-permute-start.1 = (bf16[2,32,1024]{2,1,0:T(8,128)(2,1)S(1)}, bf16[2,32,1024]{2,1,0:T(8,128)(2,1)S(1)}, u32[]{:S(2)}, u32[]{:S(2)}) collective-permute-start(bf16[2,32,1024]{2,1,0:T(8,128)(2,1)S(1)} %get-tuple-element.31), channel_id=1, source_target_pairs={{0,95},{1,0},{2,1},{3,2},{4,3},{5,4},{6,5},{7,6},{8,7},{9,8},{10,9... | collective-permute-start | bytes 393224 | tf_op jit(solution)/shard_map/ppermute | solution.py:232
  26.3 0.0 copy-start.5
  26.3 0.7 copy-done.5
  27.0 0.0 copy-done.1
  27.0 0.0 copy-start.2
  27.0 1.0 copy-done.2
  28.0 0.3 prepare.1
  28.4 0.6 copy-done.4
  29.0 0.0 copy-start.7
  29.0 0.6 copy-done.7
  29.6 0.1 dynamic_slice.7
  29.7 0.0 collective-permute-done.low
  29.7 0.0 collective-permute-done.1.high
  29.7 0.0 copy-done.3
  29.7 2.2 %forward.1 = (f32[2,192,128]{2,1,0:T(8,128)S(1)}, bf16[2,128,512]{2,1,0:T(8,128)(2,1)S(1)}, bf16[2,128,512]{2,1,0:T(8,128)(2,1)S(1)}, f32[8,2,16,128]{3,2,1,0:T(8,128)}) custom-call(s32[1]{0:T(128)} %bitcast.3.core, f32[192,128]{1,0:T(8,128)S(1)} %get-tuple-element.19.counts, f32[2,128,128]{2,1,0:T(8,128)S(1)} %get-tuple-element.20.near, ...), custom_call_target="tpu_custom_call" | custom-call | tf_op jit(solution)/shard_map/forward/pallas_call | solution.py:190
  31.9 5.0 %all-to-all-start.3 = ((f32[8,2,16,128]{3,2,1,0:T(8,128)}), f32[8,2,16,128]{3,2,1,0:T(8,128)S(1)}, u32[]{:S(2)}, u32[]{:S(2)}) async-start(f32[8,2,16,128]{3,2,1,0:T(8,128)} %get-tuple-element.21), calls=%async_computation.3 | async-start | bytes 262144 | tf_op jit(solution)/shard_map/all_to_all | solution.py:206
  36.9 0.0 copy-done.6
  36.9 0.1 broadcast_multiply_fusion
  37.0 2.0 %collective-permute-start.2 = (bf16[2,128,512]{2,1,0:T(8,128)(2,1)S(1)}, bf16[2,128,512]{2,1,0:T(8,128)(2,1)S(1)}, u32[]{:S(2)}, u32[]{:S(2)}) collective-permute-start(bf16[2,128,512]{2,1,0:T(8,128)(2,1)S(1)} %get-tuple-element.25), channel_id=1, source_target_pairs={{0,96},{96,0},{1,97},{97,1},{2,98},{98,2},{3,99},{99,3},{4,100},{1... | collective-permute-start | bytes 786440 | tf_op jit(solution)/shard_map/ppermute | solution.py:273
  39.0 0.0 copy-done
  39.0 0.1 constant_dynamic-slice_fusion
  39.1 0.1 copy.14
  39.2 3.6 %all-to-all-done.3.rows = f32[8,2,16,128]{3,2,1,0:T(8,128)S(1)} async-done(((f32[8,2,16,128]{3,2,1,0:T(8,128)}), f32[8,2,16,128]{3,2,1,0:T(8,128)S(1)}, u32[]{:S(2)}, u32[]{:S(2)}) %all-to-all-start.3) | async-done | bytes 131104 | tf_op jit(solution)/shard_map/all_to_all | solution.py:206
  42.7 0.9 crps.1
  43.7 4.2 %all-to-all-start.4 = ((bf16[8,4,16,128]{3,2,1,0:T(8,128)(2,1)}), bf16[8,4,16,128]{3,2,1,0:T(8,128)(2,1)S(1)}, u32[]{:S(2)}, u32[]{:S(2)}) async-start(bf16[8,4,16,128]{3,2,1,0:T(8,128)(2,1)} %crps.1), calls=%async_computation.4 | async-start | bytes 262144 | tf_op jit(solution)/shard_map/all_to_all | solution.py:206
  47.9 0.0 collective-permute-done.2.got
  47.9 5.8 %all-to-all-done.4.grads = bf16[8,4,16,128]{3,2,1,0:T(8,128)(2,1)S(1)} async-done(((bf16[8,4,16,128]{3,2,1,0:T(8,128)(2,1)}), bf16[8,4,16,128]{3,2,1,0:T(8,128)(2,1)S(1)}, u32[]{:S(2)}, u32[]{:S(2)}) %all-to-all-start.4) | async-done | bytes 131104 | tf_op jit(solution)/shard_map/all_to_all | solution.py:206
  53.8 1.0 weight_term.1
  54.7 3.9 %all-to-all-start.5 = ((bf16[32,16,128]{2,1,0:T(8,128)(2,1)}), bf16[32,16,128]{2,1,0:T(8,128)(2,1)S(1)}, u32[]{:S(2)}, u32[]{:S(2)}) async-start(bf16[32,16,128]{2,1,0:T(8,128)(2,1)} %weight_term.1), calls=%async_computation.5 | async-start | bytes 262144 | tf_op jit(solution)/shard_map/all_to_all | solution.py:206
  58.6 2.5 %backward.1 = (f32[2,128,1024]{2,1,0:T(8,128)S(1)}, bf16[2,32,1024]{2,1,0:T(8,128)(2,1)S(1)}, bf16[2,32,1024]{2,1,0:T(8,128)(2,1)S(1)}) custom-call(s32[1]{0:T(128)} %bitcast.2.side, bf16[8,4,16,128]{3,2,1,0:T(8,128)(2,1)S(1)} %all-to-all-done.4.grads, f32[2,192,128]{2,1,0:T(8,128)S(1)} %get-tuple-element.22.attn, bf16[2,128,1024]{2,1,0:T(8,128)(2,1)S(1)} %copy-done.1, ...), custom_call_target="tpu_custom_call" | custom-call | tf_op jit(solution)/shard_map/backward/pallas_call | solution.py:190
  61.1 6.9 %all-to-all-done.5.terms = bf16[32,16,128]{2,1,0:T(8,128)(2,1)S(1)} async-done(((bf16[32,16,128]{2,1,0:T(8,128)(2,1)}), bf16[32,16,128]{2,1,0:T(8,128)(2,1)S(1)}, u32[]{:S(2)}, u32[]{:S(2)}) %all-to-all-start.5) | async-done | bytes 131104 | tf_op jit(solution)/shard_map/all_to_all | solution.py:206
  68.0 0.7 add_plane.1
  68.6 13.2 %all-to-all-start.6 = ((bf16[12,16,128]{2,1,0:T(8,128)(2,1)}), bf16[12,16,128]{2,1,0:T(8,128)(2,1)S(1)}, u32[]{:S(2)}, u32[]{:S(2)}) async-start(bf16[12,16,128]{2,1,0:T(8,128)(2,1)} %add_plane.1), calls=%async_computation.6 | async-start | bytes 98304 | tf_op jit(solution)/shard_map/all_to_all | solution.py:206
  81.9 3.0 %collective-permute-start.3 = (bf16[2,32,1024]{2,1,0:T(8,128)(2,1)S(1)}, bf16[2,32,1024]{2,1,0:T(8,128)(2,1)S(1)}, u32[]{:S(2)}, u32[]{:S(2)}) collective-permute-start(bf16[2,32,1024]{2,1,0:T(8,128)(2,1)S(1)} %get-tuple-element.28), channel_id=1, source_target_pairs={{0,1},{1,0},{2,3},{3,2},{4,5},{5,4},{6,7},{7,6},{8,9},{9,8},{10,11... | collective-permute-start | bytes 393224 | tf_op jit(solution)/shard_map/ppermute | solution.py:309
  84.9 9.2 %collective-permute-start.4 = (bf16[2,32,1024]{2,1,0:T(8,128)(2,1)S(1)}, bf16[2,32,1024]{2,1,0:T(8,128)(2,1)S(1)}, u32[]{:S(2)}, u32[]{:S(2)}) collective-permute-start(bf16[2,32,1024]{2,1,0:T(8,128)(2,1)S(1)} %get-tuple-element.29), channel_id=1, source_target_pairs={{0,95},{1,2},{2,1},{3,4},{4,3},{5,6},{6,5},{7,8},{8,7},{9,10},{10,... | collective-permute-start | bytes 393224 | tf_op jit(solution)/shard_map/ppermute | solution.py:308
  94.1 0.0 all-to-all-done.6.terms
  94.1 12.3 %conditional.1 = (bf16[32,16,128]{2,1,0:T(8,128)(2,1)S(1)}) conditional(s32[]{:T(128)} %bitcast.6, bf16[32,16,128]{2,1,0:T(8,128)(2,1)S(1)} %add_z.1, bf16[32,16,128]{2,1,0:T(8,128)(2,1)S(1)} %add_z.1), branch_computations={%region_0.1_spmd, %region_1.2_spmd} | conditional | bytes 1048584 | solution.py:311
  94.1 12.3 %all_to_all.34 = bf16[32,16,128]{2,1,0:T(8,128)(2,1)S(1)} all-to-all(bf16[32,16,128]{2,1,0:T(8,128)(2,1)S(1)} %param.1), channel_id=1, replica_groups=mesh['ylo'=4,'core'=2,'z'=12,'x'=4,'yhi'=2] {'x','ylo','yhi'}, dimensions={0} | all-to-all | bytes 262144 | tf_op jit(solution)/shard_map/cond/branch_1_fun/all_to_all | solution.py:206
  106.5 6.7 %collective-permute-start.5 = (bf16[32,16,128]{2,1,0:T(8,128)(2,1)S(1)}, bf16[32,16,128]{2,1,0:T(8,128)(2,1)S(1)}, u32[]{:S(2)}, u32[]{:S(2)}) collective-permute-start(bf16[32,16,128]{2,1,0:T(8,128)(2,1)S(1)} %get-tuple-element.33.mine), channel_id=1, source_target_pairs={{0,96},{96,0},{1,97},{97,1},{2,98},{98,2},{3,99},{99,3},{4,100},{1... | collective-permute-start | bytes 393224 | tf_op jit(solution)/shard_map/ppermute | solution.py:312
  113.2 0.0 collective-permute-done.3.even
  113.2 0.0 collective-permute-done.4.odd
  113.2 0.9 finish.1
  114.1 0.0 collective-permute-done.5.other
  114.2 0.8 assemble.1
  (8 shorter events, 0.1 us)
Async XLA Ops:
  0.6 38.4 %copy-start = (f32[128,100]{0,1:T(8,128)S(1)}, f32[128,100]{0,1:T(8,128)}, u32[]{:S(2)}) copy-start(f32[128,100]{0,1:T(8,128)} %param.12) | copy-start | bytes 153604
  0.6 26.3 %copy-start.1 = (bf16[2,128,1024]{2,1,0:T(8,128)(2,1)S(1)}, bf16[2,128,1024]{2,1,0:T(8,128)(2,1)}, u32[]{:S(2)}) copy-start(bf16[2,128,1024]{2,1,0:T(8,128)(2,1)} %own.5) | copy-start | bytes 1572868
  1.7 28.0 %collective-permute-start = (bf16[2,32,1024]{2,1,0:T(8,128)(2,1)S(1)}, bf16[2,32,1024]{2,1,0:T(8,128)(2,1)S(1)}, u32[]{:S(2)}, u32[]{:S(2)}) collective-permute-start(bf16[2,32,1024]{2,1,0:T(8,128)(2,1)S(1)} %get-tuple-element.32), channel_id=1, source_target_pairs={{0,1},{1,2},{2,3},{3,4},{4,5},{5,6},{6,7},{7,8},{8,9},{9,10},{10,1... | collective-permute-start | bytes 393224 | tf_op jit(solution)/shard_map/ppermute | solution.py:231
  10.0 19.7 %collective-permute-start.1 = (bf16[2,32,1024]{2,1,0:T(8,128)(2,1)S(1)}, bf16[2,32,1024]{2,1,0:T(8,128)(2,1)S(1)}, u32[]{:S(2)}, u32[]{:S(2)}) collective-permute-start(bf16[2,32,1024]{2,1,0:T(8,128)(2,1)S(1)} %get-tuple-element.31), channel_id=1, source_target_pairs={{0,95},{1,0},{2,1},{3,2},{4,3},{5,4},{6,5},{7,6},{8,7},{9,8},{10,9... | collective-permute-start | bytes 393224 | tf_op jit(solution)/shard_map/ppermute | solution.py:232
  26.3 0.7 copy-start.5
  27.0 1.0 copy-start.2
  28.0 0.9 copy-start.4
  28.0 1.7 %copy-start.3 = (bf16[2,128,1024]{2,1,0:T(8,128)(2,1)S(1)}, bf16[2,128,1024]{2,1,0:T(8,128)(2,1)}, u32[]{:S(2)}) copy-start(bf16[2,128,1024]{2,1,0:T(8,128)(2,1)} %queries.5) | copy-start | bytes 1572868
  29.0 0.7 copy-start.7
  31.9 5.0 %copy-start.6 = (f32[100]{0:T(128)S(1)}, f32[100]{0:T(128)}, u32[]{:S(2)}) copy-start(f32[100]{0:T(128)} %param.14) | copy-start | bytes 1204
  31.9 10.8 %all-to-all-start.3 = ((f32[8,2,16,128]{3,2,1,0:T(8,128)}), f32[8,2,16,128]{3,2,1,0:T(8,128)S(1)}, u32[]{:S(2)}, u32[]{:S(2)}) async-start(f32[8,2,16,128]{3,2,1,0:T(8,128)} %get-tuple-element.21), calls=%async_computation.3 | async-start | bytes 262144 | tf_op jit(solution)/shard_map/all_to_all | solution.py:206
  37.0 11.0 %collective-permute-start.2 = (bf16[2,128,512]{2,1,0:T(8,128)(2,1)S(1)}, bf16[2,128,512]{2,1,0:T(8,128)(2,1)S(1)}, u32[]{:S(2)}, u32[]{:S(2)}) collective-permute-start(bf16[2,128,512]{2,1,0:T(8,128)(2,1)S(1)} %get-tuple-element.25), channel_id=1, source_target_pairs={{0,96},{96,0},{1,97},{97,1},{2,98},{98,2},{3,99},{99,3},{4,100},{1... | collective-permute-start | bytes 786440 | tf_op jit(solution)/shard_map/ppermute | solution.py:273
  43.7 10.1 %all-to-all-start.4 = ((bf16[8,4,16,128]{3,2,1,0:T(8,128)(2,1)}), bf16[8,4,16,128]{3,2,1,0:T(8,128)(2,1)S(1)}, u32[]{:S(2)}, u32[]{:S(2)}) async-start(bf16[8,4,16,128]{3,2,1,0:T(8,128)(2,1)} %crps.1), calls=%async_computation.4 | async-start | bytes 262144 | tf_op jit(solution)/shard_map/all_to_all | solution.py:206
  54.7 13.2 %all-to-all-start.5 = ((bf16[32,16,128]{2,1,0:T(8,128)(2,1)}), bf16[32,16,128]{2,1,0:T(8,128)(2,1)S(1)}, u32[]{:S(2)}, u32[]{:S(2)}) async-start(bf16[32,16,128]{2,1,0:T(8,128)(2,1)} %weight_term.1), calls=%async_computation.5 | async-start | bytes 262144 | tf_op jit(solution)/shard_map/all_to_all | solution.py:206
  68.6 25.5 %all-to-all-start.6 = ((bf16[12,16,128]{2,1,0:T(8,128)(2,1)}), bf16[12,16,128]{2,1,0:T(8,128)(2,1)S(1)}, u32[]{:S(2)}, u32[]{:S(2)}) async-start(bf16[12,16,128]{2,1,0:T(8,128)(2,1)} %add_plane.1), calls=%async_computation.6 | async-start | bytes 98304 | tf_op jit(solution)/shard_map/all_to_all | solution.py:206
  81.9 31.3 %collective-permute-start.3 = (bf16[2,32,1024]{2,1,0:T(8,128)(2,1)S(1)}, bf16[2,32,1024]{2,1,0:T(8,128)(2,1)S(1)}, u32[]{:S(2)}, u32[]{:S(2)}) collective-permute-start(bf16[2,32,1024]{2,1,0:T(8,128)(2,1)S(1)} %get-tuple-element.28), channel_id=1, source_target_pairs={{0,1},{1,0},{2,3},{3,2},{4,5},{5,4},{6,7},{7,6},{8,9},{9,8},{10,11... | collective-permute-start | bytes 393224 | tf_op jit(solution)/shard_map/ppermute | solution.py:309
  84.9 28.3 %collective-permute-start.4 = (bf16[2,32,1024]{2,1,0:T(8,128)(2,1)S(1)}, bf16[2,32,1024]{2,1,0:T(8,128)(2,1)S(1)}, u32[]{:S(2)}, u32[]{:S(2)}) collective-permute-start(bf16[2,32,1024]{2,1,0:T(8,128)(2,1)S(1)} %get-tuple-element.29), channel_id=1, source_target_pairs={{0,95},{1,2},{2,1},{3,4},{4,3},{5,6},{6,5},{7,8},{8,7},{9,10},{10,... | collective-permute-start | bytes 393224 | tf_op jit(solution)/shard_map/ppermute | solution.py:308
  106.5 7.7 %collective-permute-start.5 = (bf16[32,16,128]{2,1,0:T(8,128)(2,1)S(1)}, bf16[32,16,128]{2,1,0:T(8,128)(2,1)S(1)}, u32[]{:S(2)}, u32[]{:S(2)}) collective-permute-start(bf16[32,16,128]{2,1,0:T(8,128)(2,1)S(1)} %get-tuple-element.33.mine), channel_id=1, source_target_pairs={{0,96},{96,0},{1,97},{97,1},{2,98},{98,2},{3,99},{99,3},{4,100},{1... | collective-permute-start | bytes 393224 | tf_op jit(solution)/shard_map/ppermute | solution.py:312

commit v6 on v5

--- a/solution.py
+++ b/solution.py
@@ -229,7 +229,7 @@
     backward = [(i, (i - 1) % shards) for i in range(shards)]
 
     low = lax.ppermute(latents[:, nodes - reach :], SHARD, forward)
-    high = lax.ppermute(latents[:, :reach], SHARD, backward)
+    high = lax.ppermute(lax.optimization_barrier(latents)[:, :reach], SHARD, backward)
 
     first = lax.axis_index(SHARD) * nodes
     index = (neighbours.T - first + reach) % (nodes * shards)

time: 116 us -> 117 us (level)
  transfers between devices with their start and end apart: 10 -> 10, of which waited for: 3 -> 3; matrix products, arithmetic and copies ran while one was open for 0% -> 1% of each run, Pallas kernels for 4% -> 4%
where the time goes in v6:
time: 117 us; the launch traced here: 116 us
  starting transfers between devices  72 us (62%)
  waiting for transfers between devices  16.3 us (14%)
  blocking collectives  12.3 us (11%)
  Pallas kernels  9.26 us (8%)
  local copies, waits for them, and re-layouts  5.12 us (4%)
    all_to_all x4, starting transfers between devices, exchange(): return lax.all_to_all(x, axes, 0, 0, tiled=True)  26.6 us
    all_to_all x4, waiting for transfers between devices, exchange(): return lax.all_to_all(x, axes, 0, 0, tiled=True)  16.3 us
    ppermute x1, starting transfers between devices, local(): lax.ppermute(lax.optimization_barrier(latents)[:, :reach], SHARD, backward)  16.2 us
    all_to_all x1, blocking collectives, exchange(): return lax.all_to_all(x, axes, 0, 0, tiled=True)  12.3 us
    pallas_call x9, Pallas kernels, call(): pl.pallas_call(kernel, out_shape=out_shape, in_specs=[smem] * scalars + [...  9.26 us
    ppermute x1, starting transfers between devices, local(): odd_back = lax.ppermute(odd_part, SHARD, odd_pairs)  9.16 us
    ppermute x1, starting transfers between devices, local(): low = lax.ppermute(latents[:, nodes - reach:], SHARD, forward)  8.28 us
    ppermute x1, starting transfers between devices, local(): other = lax.ppermute(mine, 'core', swap)  6.73 us
  transfers between devices with their start and end apart: 10, of which 3 were waited for; matrix products, arithmetic and copies ran while one was open for 1% of the time, Pallas kernels for 4%

profile of v6, /device:TPU:1, one launch (start us, length us, event | category | flops | bytes accessed | tf_op | source)
XLA Modules:
  0.0 116.0 jit_solution(14172764607443169772)
XLA Ops:
  0.6 0.0 copy-start
  0.6 0.0 copy-start.1
  0.7 1.0 slice.9
  1.6 8.3 %collective-permute-start = (bf16[2,32,1024]{2,1,0:T(8,128)(2,1)S(1)}, bf16[2,32,1024]{2,1,0:T(8,128)(2,1)S(1)}, u32[]{:S(2)}, u32[]{:S(2)}) collective-permute-start(bf16[2,32,1024]{2,1,0:T(8,128)(2,1)S(1)} %slice.9), channel_id=1, source_target_pairs={{0,1},{1,2},{2,3},{3,4},{4,5},{5,6},{6,7},{7,8},{8,9},{9,10},{10,1... | collective-permute-start | bytes 393224 | tf_op jit(solution)/shard_map/ppermute | solution.py:231
  9.9 0.9 slice.12
  10.8 16.2 %collective-permute-start.1 = (bf16[2,32,1024]{2,1,0:T(8,128)(2,1)S(1)}, bf16[2,32,1024]{2,1,0:T(8,128)(2,1)S(1)}, u32[]{:S(2)}, u32[]{:S(2)}) collective-permute-start(bf16[2,32,1024]{2,1,0:T(8,128)(2,1)S(1)} %slice.12), channel_id=1, source_target_pairs={{0,95},{1,0},{2,1},{3,2},{4,3},{5,4},{6,5},{7,6},{8,7},{9,8},{10,9... | collective-permute-start | bytes 393224 | tf_op jit(solution)/shard_map/ppermute | solution.py:232
  27.1 0.0 copy-start.5
  27.1 0.7 copy-done.5
  27.8 0.0 copy-done.1
  27.8 0.0 copy-start.2
  27.8 1.0 copy-done.2
  28.9 0.3 prepare.1
  29.2 0.6 copy-done.4
  29.8 0.0 copy-start.7
  29.8 0.6 copy-done.7
  30.5 0.1 dynamic_slice.7
  30.6 0.0 collective-permute-done.low
  30.6 0.0 collective-permute-done.1.high
  30.6 0.0 copy-done.3
  30.6 2.2 %forward.1 = (f32[2,192,128]{2,1,0:T(8,128)S(1)}, bf16[2,128,512]{2,1,0:T(8,128)(2,1)S(1)}, bf16[2,128,512]{2,1,0:T(8,128)(2,1)S(1)}, f32[8,2,16,128]{3,2,1,0:T(8,128)}) custom-call(s32[1]{0:T(128)} %bitcast.3.core, f32[192,128]{1,0:T(8,128)S(1)} %get-tuple-element.19.counts, f32[2,128,128]{2,1,0:T(8,128)S(1)} %get-tuple-element.20.near, ...), custom_call_target="tpu_custom_call" | custom-call | tf_op jit(solution)/shard_map/forward/pallas_call | solution.py:190
  32.8 4.4 %all-to-all-start.3 = ((f32[8,2,16,128]{3,2,1,0:T(8,128)}), f32[8,2,16,128]{3,2,1,0:T(8,128)S(1)}, u32[]{:S(2)}, u32[]{:S(2)}) async-start(f32[8,2,16,128]{3,2,1,0:T(8,128)} %get-tuple-element.21), calls=%async_computation.3 | async-start | bytes 262144 | tf_op jit(solution)/shard_map/all_to_all | solution.py:206
  37.1 0.0 copy-done.6
  37.1 0.1 broadcast_multiply_fusion
  37.2 2.0 %collective-permute-start.2 = (bf16[2,128,512]{2,1,0:T(8,128)(2,1)S(1)}, bf16[2,128,512]{2,1,0:T(8,128)(2,1)S(1)}, u32[]{:S(2)}, u32[]{:S(2)}) collective-permute-start(bf16[2,128,512]{2,1,0:T(8,128)(2,1)S(1)} %get-tuple-element.25), channel_id=1, source_target_pairs={{0,96},{96,0},{1,97},{97,1},{2,98},{98,2},{3,99},{99,3},{4,100},{1... | collective-permute-start | bytes 786440 | tf_op jit(solution)/shard_map/ppermute | solution.py:273
  39.2 0.1 constant_dynamic-slice_fusion
  39.3 0.1 copy.14
  39.4 3.6 %all-to-all-done.3.rows = f32[8,2,16,128]{3,2,1,0:T(8,128)S(1)} async-done(((f32[8,2,16,128]{3,2,1,0:T(8,128)}), f32[8,2,16,128]{3,2,1,0:T(8,128)S(1)}, u32[]{:S(2)}, u32[]{:S(2)}) %all-to-all-start.3) | async-done | bytes 131104 | tf_op jit(solution)/shard_map/all_to_all | solution.py:206
  43.0 0.9 crps.1
  43.9 4.2 %all-to-all-start.4 = ((bf16[8,4,16,128]{3,2,1,0:T(8,128)(2,1)}), bf16[8,4,16,128]{3,2,1,0:T(8,128)(2,1)S(1)}, u32[]{:S(2)}, u32[]{:S(2)}) async-start(bf16[8,4,16,128]{3,2,1,0:T(8,128)(2,1)} %crps.1), calls=%async_computation.4 | async-start | bytes 262144 | tf_op jit(solution)/shard_map/all_to_all | solution.py:206
  48.1 0.0 collective-permute-done.2.got
  48.2 5.8 %all-to-all-done.4.grads = bf16[8,4,16,128]{3,2,1,0:T(8,128)(2,1)S(1)} async-done(((bf16[8,4,16,128]{3,2,1,0:T(8,128)(2,1)}), bf16[8,4,16,128]{3,2,1,0:T(8,128)(2,1)S(1)}, u32[]{:S(2)}, u32[]{:S(2)}) %all-to-all-start.4) | async-done | bytes 131104 | tf_op jit(solution)/shard_map/all_to_all | solution.py:206
  54.0 1.0 weight_term.1
  55.0 3.9 %all-to-all-start.5 = ((bf16[32,16,128]{2,1,0:T(8,128)(2,1)}), bf16[32,16,128]{2,1,0:T(8,128)(2,1)S(1)}, u32[]{:S(2)}, u32[]{:S(2)}) async-start(bf16[32,16,128]{2,1,0:T(8,128)(2,1)} %weight_term.1), calls=%async_computation.5 | async-start | bytes 262144 | tf_op jit(solution)/shard_map/all_to_all | solution.py:206
  58.8 2.4 %backward.1 = (f32[2,128,1024]{2,1,0:T(8,128)S(1)}, bf16[2,32,1024]{2,1,0:T(8,128)(2,1)S(1)}, bf16[2,32,1024]{2,1,0:T(8,128)(2,1)S(1)}) custom-call(s32[1]{0:T(128)} %bitcast.2.side, bf16[8,4,16,128]{3,2,1,0:T(8,128)(2,1)S(1)} %all-to-all-done.4.grads, f32[2,192,128]{2,1,0:T(8,128)S(1)} %get-tuple-element.22.attn, bf16[2,128,1024]{2,1,0:T(8,128)(2,1)S(1)} %copy-done.1, ...), custom_call_target="tpu_custom_call" | custom-call | tf_op jit(solution)/shard_map/backward/pallas_call | solution.py:190
  61.3 6.9 %all-to-all-done.5.terms = bf16[32,16,128]{2,1,0:T(8,128)(2,1)S(1)} async-done(((bf16[32,16,128]{2,1,0:T(8,128)(2,1)}), bf16[32,16,128]{2,1,0:T(8,128)(2,1)S(1)}, u32[]{:S(2)}, u32[]{:S(2)}) %all-to-all-start.5) | async-done | bytes 131104 | tf_op jit(solution)/shard_map/all_to_all | solution.py:206
  68.2 0.7 add_plane.1
  68.8 14.1 %all-to-all-start.6 = ((bf16[12,16,128]{2,1,0:T(8,128)(2,1)}), bf16[12,16,128]{2,1,0:T(8,128)(2,1)S(1)}, u32[]{:S(2)}, u32[]{:S(2)}) async-start(bf16[12,16,128]{2,1,0:T(8,128)(2,1)} %add_plane.1), calls=%async_computation.6 | async-start | bytes 98304 | tf_op jit(solution)/shard_map/all_to_all | solution.py:206
  83.0 3.0 %collective-permute-start.3 = (bf16[2,32,1024]{2,1,0:T(8,128)(2,1)S(1)}, bf16[2,32,1024]{2,1,0:T(8,128)(2,1)S(1)}, u32[]{:S(2)}, u32[]{:S(2)}) collective-permute-start(bf16[2,32,1024]{2,1,0:T(8,128)(2,1)S(1)} %get-tuple-element.28), channel_id=1, source_target_pairs={{0,1},{1,0},{2,3},{3,2},{4,5},{5,4},{6,7},{7,6},{8,9},{9,8},{10,11... | collective-permute-start | bytes 393224 | tf_op jit(solution)/shard_map/ppermute | solution.py:309
  86.0 9.2 %collective-permute-start.4 = (bf16[2,32,1024]{2,1,0:T(8,128)(2,1)S(1)}, bf16[2,32,1024]{2,1,0:T(8,128)(2,1)S(1)}, u32[]{:S(2)}, u32[]{:S(2)}) collective-permute-start(bf16[2,32,1024]{2,1,0:T(8,128)(2,1)S(1)} %get-tuple-element.29), channel_id=1, source_target_pairs={{0,95},{1,2},{2,1},{3,4},{4,3},{5,6},{6,5},{7,8},{8,7},{9,10},{10,... | collective-permute-start | bytes 393224 | tf_op jit(solution)/shard_map/ppermute | solution.py:308
  95.2 0.0 all-to-all-done.6.terms
  95.2 12.3 %conditional.1 = (bf16[32,16,128]{2,1,0:T(8,128)(2,1)S(1)}) conditional(s32[]{:T(128)} %bitcast.6, bf16[32,16,128]{2,1,0:T(8,128)(2,1)S(1)} %add_z.1, bf16[32,16,128]{2,1,0:T(8,128)(2,1)S(1)} %add_z.1), branch_computations={%region_0.1_spmd, %region_1.2_spmd} | conditional | bytes 1048584 | solution.py:311
  95.2 12.3 %all_to_all.34 = bf16[32,16,128]{2,1,0:T(8,128)(2,1)S(1)} all-to-all(bf16[32,16,128]{2,1,0:T(8,128)(2,1)S(1)} %param.1), channel_id=1, replica_groups=mesh['ylo'=4,'core'=2,'z'=12,'x'=4,'yhi'=2] {'x','ylo','yhi'}, dimensions={0} | all-to-all | bytes 262144 | tf_op jit(solution)/shard_map/cond/branch_1_fun/all_to_all | solution.py:206
  107.6 6.7 %collective-permute-start.5 = (bf16[32,16,128]{2,1,0:T(8,128)(2,1)S(1)}, bf16[32,16,128]{2,1,0:T(8,128)(2,1)S(1)}, u32[]{:S(2)}, u32[]{:S(2)}) collective-permute-start(bf16[32,16,128]{2,1,0:T(8,128)(2,1)S(1)} %get-tuple-element.31.mine), channel_id=1, source_target_pairs={{0,96},{96,0},{1,97},{97,1},{2,98},{98,2},{3,99},{99,3},{4,100},{1... | collective-permute-start | bytes 393224 | tf_op jit(solution)/shard_map/ppermute | solution.py:312
  114.3 0.0 collective-permute-done.3.even
  114.3 0.0 collective-permute-done.4.odd
  114.3 0.9 finish.1
  115.2 0.0 collective-permute-done.5.other
  115.3 0.8 assemble.1
  (9 shorter events, 0.1 us)
Async XLA Ops:
  0.6 38.6 %copy-start = (f32[128,100]{0,1:T(8,128)S(1)}, f32[128,100]{0,1:T(8,128)}, u32[]{:S(2)}) copy-start(f32[128,100]{0,1:T(8,128)} %param.12) | copy-start | bytes 153604
  0.6 27.2 %copy-start.1 = (bf16[2,128,1024]{2,1,0:T(8,128)(2,1)S(1)}, bf16[2,128,1024]{2,1,0:T(8,128)(2,1)}, u32[]{:S(2)}) copy-start(bf16[2,128,1024]{2,1,0:T(8,128)(2,1)} %own.5) | copy-start | bytes 1572868
  1.6 28.9 %collective-permute-start = (bf16[2,32,1024]{2,1,0:T(8,128)(2,1)S(1)}, bf16[2,32,1024]{2,1,0:T(8,128)(2,1)S(1)}, u32[]{:S(2)}, u32[]{:S(2)}) collective-permute-start(bf16[2,32,1024]{2,1,0:T(8,128)(2,1)S(1)} %slice.9), channel_id=1, source_target_pairs={{0,1},{1,2},{2,3},{3,4},{4,5},{5,6},{6,7},{7,8},{8,9},{9,10},{10,1... | collective-permute-start | bytes 393224 | tf_op jit(solution)/shard_map/ppermute | solution.py:231
  10.8 19.7 %collective-permute-start.1 = (bf16[2,32,1024]{2,1,0:T(8,128)(2,1)S(1)}, bf16[2,32,1024]{2,1,0:T(8,128)(2,1)S(1)}, u32[]{:S(2)}, u32[]{:S(2)}) collective-permute-start(bf16[2,32,1024]{2,1,0:T(8,128)(2,1)S(1)} %slice.12), channel_id=1, source_target_pairs={{0,95},{1,0},{2,1},{3,2},{4,3},{5,4},{6,5},{7,6},{8,7},{9,8},{10,9... | collective-permute-start | bytes 393224 | tf_op jit(solution)/shard_map/ppermute | solution.py:232
  27.1 0.7 copy-start.5
  27.8 1.0 copy-start.2
  28.9 0.9 copy-start.4
  28.9 1.7 %copy-start.3 = (bf16[2,128,1024]{2,1,0:T(8,128)(2,1)S(1)}, bf16[2,128,1024]{2,1,0:T(8,128)(2,1)}, u32[]{:S(2)}) copy-start(bf16[2,128,1024]{2,1,0:T(8,128)(2,1)} %queries.5) | copy-start | bytes 1572868
  29.8 0.7 copy-start.7
  32.8 4.4 %copy-start.6 = (f32[100]{0:T(128)S(1)}, f32[100]{0:T(128)}, u32[]{:S(2)}) copy-start(f32[100]{0:T(128)} %param.14) | copy-start | bytes 1204
  32.8 10.2 %all-to-all-start.3 = ((f32[8,2,16,128]{3,2,1,0:T(8,128)}), f32[8,2,16,128]{3,2,1,0:T(8,128)S(1)}, u32[]{:S(2)}, u32[]{:S(2)}) async-start(f32[8,2,16,128]{3,2,1,0:T(8,128)} %get-tuple-element.21), calls=%async_computation.3 | async-start | bytes 262144 | tf_op jit(solution)/shard_map/all_to_all | solution.py:206
  37.2 11.0 %collective-permute-start.2 = (bf16[2,128,512]{2,1,0:T(8,128)(2,1)S(1)}, bf16[2,128,512]{2,1,0:T(8,128)(2,1)S(1)}, u32[]{:S(2)}, u32[]{:S(2)}) collective-permute-start(bf16[2,128,512]{2,1,0:T(8,128)(2,1)S(1)} %get-tuple-element.25), channel_id=1, source_target_pairs={{0,96},{96,0},{1,97},{97,1},{2,98},{98,2},{3,99},{99,3},{4,100},{1... | collective-permute-start | bytes 786440 | tf_op jit(solution)/shard_map/ppermute | solution.py:273
  43.9 10.1 %all-to-all-start.4 = ((bf16[8,4,16,128]{3,2,1,0:T(8,128)(2,1)}), bf16[8,4,16,128]{3,2,1,0:T(8,128)(2,1)S(1)}, u32[]{:S(2)}, u32[]{:S(2)}) async-start(bf16[8,4,16,128]{3,2,1,0:T(8,128)(2,1)} %crps.1), calls=%async_computation.4 | async-start | bytes 262144 | tf_op jit(solution)/shard_map/all_to_all | solution.py:206
  55.0 13.2 %all-to-all-start.5 = ((bf16[32,16,128]{2,1,0:T(8,128)(2,1)}), bf16[32,16,128]{2,1,0:T(8,128)(2,1)S(1)}, u32[]{:S(2)}, u32[]{:S(2)}) async-start(bf16[32,16,128]{2,1,0:T(8,128)(2,1)} %weight_term.1), calls=%async_computation.5 | async-start | bytes 262144 | tf_op jit(solution)/shard_map/all_to_all | solution.py:206
  68.8 26.4 %all-to-all-start.6 = ((bf16[12,16,128]{2,1,0:T(8,128)(2,1)}), bf16[12,16,128]{2,1,0:T(8,128)(2,1)S(1)}, u32[]{:S(2)}, u32[]{:S(2)}) async-start(bf16[12,16,128]{2,1,0:T(8,128)(2,1)} %add_plane.1), calls=%async_computation.6 | async-start | bytes 98304 | tf_op jit(solution)/shard_map/all_to_all | solution.py:206
  83.0 31.3 %collective-permute-start.3 = (bf16[2,32,1024]{2,1,0:T(8,128)(2,1)S(1)}, bf16[2,32,1024]{2,1,0:T(8,128)(2,1)S(1)}, u32[]{:S(2)}, u32[]{:S(2)}) collective-permute-start(bf16[2,32,1024]{2,1,0:T(8,128)(2,1)S(1)} %get-tuple-element.28), channel_id=1, source_target_pairs={{0,1},{1,0},{2,3},{3,2},{4,5},{5,4},{6,7},{7,6},{8,9},{9,8},{10,11... | collective-permute-start | bytes 393224 | tf_op jit(solution)/shard_map/ppermute | solution.py:309
  86.0 28.3 %collective-permute-start.4 = (bf16[2,32,1024]{2,1,0:T(8,128)(2,1)S(1)}, bf16[2,32,1024]{2,1,0:T(8,128)(2,1)S(1)}, u32[]{:S(2)}, u32[]{:S(2)}) collective-permute-start(bf16[2,32,1024]{2,1,0:T(8,128)(2,1)S(1)} %get-tuple-element.29), channel_id=1, source_target_pairs={{0,95},{1,2},{2,1},{3,4},{4,3},{5,6},{6,5},{7,8},{8,7},{9,10},{10,... | collective-permute-start | bytes 393224 | tf_op jit(solution)/shard_map/ppermute | solution.py:308
  107.6 7.7 %collective-permute-start.5 = (bf16[32,16,128]{2,1,0:T(8,128)(2,1)S(1)}, bf16[32,16,128]{2,1,0:T(8,128)(2,1)S(1)}, u32[]{:S(2)}, u32[]{:S(2)}) collective-permute-start(bf16[32,16,128]{2,1,0:T(8,128)(2,1)S(1)} %get-tuple-element.31.mine), channel_id=1, source_target_pairs={{0,96},{96,0},{1,97},{97,1},{2,98},{98,2},{3,99},{99,3},{4,100},{1... | collective-permute-start | bytes 393224 | tf_op jit(solution)/shard_map/ppermute | solution.py:312
